TPU v7x, 512 devices: a whole 4x4x16 slice. The times are simulated.
512 devices in a mesh: dp: 8 (over x, core), expert: 64 (over z, y).
Axes of the slice: x: 4, y: 4, z: 16, core: 2. Of those that a mesh axis runs over, the one named last changes fastest.
Arguments:
- tokens: bfloat16 [65536, 1024], P(('dp', 'expert')), may hold values from -6 to 6
- expert_ids: int32 [65536, 4], P(('dp', 'expert')), may hold values from 0 to 127, all different within a row; in each aligned block of 128 rows (0 to 127, 128 to 255, ...) at most 5 rows name the same one
- gates: bfloat16 [65536, 4], P(('dp', 'expert')), may hold values from 0.099609375 to 1
- w_up: bfloat16 [128, 1024, 512], P('expert', 'dp'), may hold values from -0.1875 to 0.1875
- w_down: bfloat16 [128, 512, 1024], P('expert', None, 'dp'), may hold values from -0.25 to 0.25
- out_grad: bfloat16 [65536, 1024], P(('dp', 'expert')), may hold values from -6 to 6
Outputs:
- mixed: bfloat16 [65536, 1024], P(('dp', 'expert'))
- tokens_grad: bfloat16 [65536, 1024], P(('dp', 'expert'))
- gate_grad: bfloat16 [65536, 4], P(('dp', 'expert'))
- up_grad: float32 [128, 1024, 512], P('expert', 'dp')
- down_grad: float32 [128, 512, 1024], P('expert', None, 'dp')
Inputs may be any that keep to these rules, and one draw needn't show every extreme that they name: `expert_ids`: A token's 4 experts differ. Within the tokens of one device (aligned blocks of 128 tokens) no expert is chosen more than 5 times, and in every draw some expert is chosen exactly 5 times there; every expert is chosen somewhere.
All inputs are finite; a program needn't handle non-finite values.
Results may differ from a plain program's by a relative error of at most 0.017.
Values may be sent and summed in bfloat16 or wider, within the bound.
A program may use at most 64 MiB of HBM per device.

v0:
```python
import jax
import jax.numpy as jnp
from jax import lax
from jax.sharding import PartitionSpec as P


def gelu(value):
    return 0.5 * value * (1.0 + jnp.tanh(0.7978845608 * (value + 0.044715 * value * value * value)))


def shards(tokens, expert_ids, gates, w_up, w_down, out_grad):
    tok_count, width = tokens.shape
    choose = expert_ids.shape[1]
    peers = lax.axis_size("expert")
    local = w_up.shape[0]
    experts = local * peers
    capacity = tok_count * choose * 5 // (4 * experts)
    slots = experts * capacity
    flat_ids = expert_ids.reshape(-1)
    onehot = (flat_ids[:, None] == jnp.arange(experts, dtype=jnp.int32)[None, :]).astype(jnp.int32)
    ranks = jnp.sum((jnp.cumsum(onehot, axis=0) - onehot) * onehot, axis=1)
    target = (flat_ids * capacity + ranks).reshape(tok_count, choose)
    select = jnp.arange(slots, dtype=jnp.int32)[:, None, None] == target[None, :, :]
    placing = jnp.any(select, axis=2).astype(jnp.bfloat16)
    weighting = jnp.sum(
        jnp.where(select, gates[None, :, :].astype(jnp.float32), 0.0), axis=2
    ).astype(jnp.bfloat16)
    joined = jnp.concatenate([tokens, out_grad], axis=1)
    packed = jnp.dot(placing, joined, preferred_element_type=jnp.float32).astype(jnp.bfloat16)
    packed = packed.reshape(peers, local, capacity, 2 * width)
    slot_gate = (
        jnp.sum(weighting.astype(jnp.float32), axis=1)
        .astype(jnp.bfloat16)
        .reshape(peers, local, capacity)
    )
    arrived, arrived_gate = (
        lax.all_to_all(packed, "expert", split_axis=0, concat_axis=0, tiled=True),
        lax.all_to_all(slot_gate, "expert", split_axis=0, concat_axis=0, tiled=True),
    )
    rows_in = arrived[..., :width]
    cotan_in = arrived[..., width:]
    scaled = (arrived_gate.astype(jnp.float32)[..., None] * cotan_in.astype(jnp.float32)).astype(
        jnp.bfloat16
    )
    full_up, full_down = (
        lax.all_gather(w_up, "dp", axis=1, tiled=True),
        lax.all_gather(w_down, "dp", axis=2, tiled=True),
    )
    pre = jnp.einsum("secd,edf->secf", rows_in, full_up, preferred_element_type=jnp.float32)
    act, pullback = jax.vjp(gelu, pre)
    act_b = act.astype(jnp.bfloat16)
    outs = jnp.einsum(
        "secf,efd->secd", act_b, full_down, preferred_element_type=jnp.float32
    ).astype(jnp.bfloat16)
    slot_dot = jnp.sum(cotan_in.astype(jnp.float32) * outs.astype(jnp.float32), axis=3).astype(
        jnp.bfloat16
    )
    act_grad = jnp.einsum("secd,efd->secf", scaled, full_down, preferred_element_type=jnp.float32)
    pre_grad = pullback(act_grad)[0].astype(jnp.bfloat16)
    row_grad = jnp.einsum(
        "secf,edf->secd", pre_grad, full_up, preferred_element_type=jnp.float32
    ).astype(jnp.bfloat16)
    part_up = jnp.einsum("secd,secf->edf", rows_in, pre_grad, preferred_element_type=jnp.float32)
    part_down = jnp.einsum("secf,secd->efd", act_b, scaled, preferred_element_type=jnp.float32)
    up_grad, down_grad = (
        lax.psum_scatter(
            part_up.astype(jnp.bfloat16), "dp", scatter_dimension=1, tiled=True
        ).astype(jnp.float32),
        lax.psum_scatter(
            part_down.astype(jnp.bfloat16), "dp", scatter_dimension=2, tiled=True
        ).astype(jnp.float32),
    )
    outs_home, dots_home, grads_home = (
        lax.all_to_all(outs, "expert", split_axis=0, concat_axis=0, tiled=True),
        lax.all_to_all(slot_dot, "expert", split_axis=0, concat_axis=0, tiled=True),
        lax.all_to_all(row_grad, "expert", split_axis=0, concat_axis=0, tiled=True),
    )
    flat_out = outs_home.reshape(slots, width)
    flat_grad = grads_home.reshape(slots, width)
    mixed = jnp.dot(weighting.T, flat_out, preferred_element_type=jnp.float32).astype(jnp.bfloat16)
    tokens_grad = jnp.dot(placing.T, flat_grad, preferred_element_type=jnp.float32).astype(
        jnp.bfloat16
    )
    gate_grad = dots_home.reshape(slots)[target]
    return (mixed, tokens_grad, gate_grad, up_grad, down_grad)


def solution(mesh):
    return jax.shard_map(
        shards,
        mesh=mesh,
        in_specs=(
            P(("dp", "expert"), None),
            P(("dp", "expert"), None),
            P(("dp", "expert"), None),
            P("expert", "dp", None),
            P("expert", None, "dp"),
            P(("dp", "expert"), None),
        ),
        out_specs=(
            P(("dp", "expert"), None),
            P(("dp", "expert"), None),
            P(("dp", "expert"), None),
            P("expert", "dp", None),
            P("expert", None, "dp"),
        ),
        check_vma=False,
    )
```

profile of v0, /device:TPU:1, one launch (start us, length us, event | category | flops | bytes accessed | tf_op | source)
XLA Modules:
  0.0 359.3 jit_solution(326090124585504254)
XLA Ops:
  7.2 0.8 copy.111
  8.4 0.2 fusion.46
  8.7 0.2 fusion.45
  9.3 0.7 copy-done.2
  10.1 0.9 reshape.57
  11.0 19.3 %all-to-all-start.2 = ((bf16[64,2,5]{2,1,0:T(2,128)(2,1)}), bf16[64,2,5]{2,1,0:T(2,128)(2,1)S(1)}, u32[]{:S(2)}, u32[]{:S(2)}) async-start(bf16[64,2,5]{2,1,0:T(2,128)(2,1)} %reshape.57), calls=%async_computation.2 | async-start | bytes 65536 | tf_op jit(solution)/shard_map/all_to_all | solution.py:38
  30.5 0.8 convolution_convert_fusion
  31.3 2.8 reshape.55
  34.1 6.9 %copy.116 = bf16[64,2,5,2048]{3,1,2,0:T(2,128)(2,1)} copy(bf16[64,2,5,2048]{3,2,1,0:T(8,128)(2,1)} %reshape.55) | data formatting | bytes 5242880 | tf_op jit(solution)/shard_map/reshape | solution.py:30
  41.1 2.6 all-to-all-done.2
  43.7 11.9 %all-to-all-start = ((bf16[64,2,5,2048]{3,1,2,0:T(2,128)(2,1)}), bf16[64,2,5,2048]{3,1,2,0:T(2,128)(2,1)S(1)}, u32[]{:S(2)}, u32[]{:S(2)}) async-start(bf16[64,2,5,2048]{3,1,2,0:T(2,128)(2,1)} %copy.116), calls=%async_computation | async-start | bytes 5242880 | tf_op jit(solution)/shard_map/all_to_all | solution.py:37
  55.6 0.7 all-gather.3.cloned.1.call-update
  56.4 0.7 all-gather.5.cloned.1.call-update
  57.2 114.5 %all-to-all-done = bf16[64,2,5,2048]{3,1,2,0:T(2,128)(2,1)S(1)} async-done(((bf16[64,2,5,2048]{3,1,2,0:T(2,128)(2,1)}), bf16[64,2,5,2048]{3,1,2,0:T(2,128)(2,1)S(1)}, u32[]{:S(2)}, u32[]{:S(2)}) %all-to-all-start) | async-done | bytes 2621472 | tf_op jit(solution)/shard_map/all_to_all | solution.py:37
  171.7 3.3 fusion.51
  175.0 2.9 fusion.19
  178.0 4.3 %fusion.1 = (bf16[64,2,5]{0,2,1:T(8,128)(2,1)S(1)}, bf16[64,2,5,1024]{3,0,2,1:T(8,128)(2,1)}) fusion(bf16[64,2,5,1024]{3,1,2,0:T(2,128)(2,1)S(1)} %copy-done.3, bf16[2,512,1024]{2,1,0:T(8,128)(2,1)} %all-gather.5.cloned.1.call-done, f32[64,2,5,512]{3,0,2,1:T(8,128)S(1)} %fusion.19), kind=kOutput, calls=%fused_computation.7 | convolution fusion | flops 677313920 | bytes 6030592 | tf_op jit(solution)/shard_map/secf,efd->secd/dot_general | solution.py:52
  182.3 0.7 copy.126
  183.0 11.7 %all-to-all-start.4 = ((bf16[64,2,5]{2,1,0:T(2,128)(2,1)}), bf16[64,2,5]{2,1,0:T(2,128)(2,1)S(1)}, u32[]{:S(2)}, u32[]{:S(2)}) async-start(bf16[64,2,5]{2,1,0:T(2,128)(2,1)} %copy.126), calls=%async_computation.4 | async-start | bytes 65536 | tf_op jit(solution)/shard_map/all_to_all | solution.py:75
  194.8 3.6 %fusion.31 = bf16[64,2,5,512]{3,0,2,1:T(8,128)(2,1)S(1)} fusion(f32[64,2,5,512]{3,0,2,1:T(8,128)S(1)} %fusion.19, bf16[2,512,1024]{2,1,0:T(8,128)(2,1)} %all-gather.5.cloned.1.call-done, f32[64,2,5]{0,2,1:T(8,128)S(1)} %copy.121, bf16[64,2,5,1024]{3,1,2,0:T(2,128)(2,1)S(1)} %copy-done.3), kind=kOutput, calls=%fused_computation.29 | convolution fusion | flops 680919040 | bytes 5376512 | tf_op jit(solution)/shard_map/secd,efd->secf/dot_general | solution.py:58
  198.4 0.9 fusion.22
  199.3 2.4 copy.123
  201.7 6.4 %all-to-all-done.4 = bf16[64,2,5]{2,1,0:T(2,128)(2,1)S(1)} async-done(((bf16[64,2,5]{2,1,0:T(2,128)(2,1)}), bf16[64,2,5]{2,1,0:T(2,128)(2,1)S(1)}, u32[]{:S(2)}, u32[]{:S(2)}) %all-to-all-start.4) | async-done | bytes 1312 | tf_op jit(solution)/shard_map/all_to_all | solution.py:75
  208.2 8.1 %all-to-all-start.3 = ((bf16[64,2,5,1024]{3,1,2,0:T(2,128)(2,1)}), bf16[64,2,5,1024]{3,1,2,0:T(2,128)(2,1)S(1)}, u32[]{:S(2)}, u32[]{:S(2)}) async-start(bf16[64,2,5,1024]{3,1,2,0:T(2,128)(2,1)} %copy.123), calls=%async_computation.3 | async-start | bytes 2621440 | tf_op jit(solution)/shard_map/all_to_all | solution.py:76
  216.3 4.2 %bitcast_convert_fusion = bf16[2,512,1024]{2,1,0:T(8,128)(2,1)} fusion(f32[64,2,5]{0,2,1:T(8,128)S(1)} %copy.121, bf16[64,2,5,1024]{3,1,2,0:T(2,128)(2,1)S(1)} %copy-done.3, f32[64,2,5,512]{3,0,2,1:T(8,128)} %copy-done.4), kind=kOutput, calls=%fused_computation.1 | convolution fusion | flops 677052416 | bytes 4721152 | tf_op jit(solution)/shard_map/secf,secd->efd/dot_general | solution.py:64
  220.6 4.8 %copy.133 = bf16[2,512,1024]{1,0,2:T(2,128)(2,1)S(1)} copy(bf16[2,512,1024]{2,1,0:T(8,128)(2,1)} %bitcast_convert_fusion) | data formatting | bytes 4194304
  225.4 1.9 copy.137
  227.3 1.3 copy-done.5
  228.6 2.4 copy.118
  231.0 46.6 %all-to-all-done.3 = bf16[64,2,5,1024]{3,1,2,0:T(2,128)(2,1)S(1)} async-done(((bf16[64,2,5,1024]{3,1,2,0:T(2,128)(2,1)}), bf16[64,2,5,1024]{3,1,2,0:T(2,128)(2,1)S(1)}, u32[]{:S(2)}, u32[]{:S(2)}) %all-to-all-start.3) | async-done | bytes 1310752 | tf_op jit(solution)/shard_map/all_to_all | solution.py:76
  277.7 9.3 %all-to-all-start.1 = ((bf16[64,2,5,1024]{3,1,2,0:T(2,128)(2,1)}), bf16[64,2,5,1024]{3,1,2,0:T(2,128)(2,1)}, u32[]{:S(2)}, u32[]{:S(2)}) async-start(bf16[64,2,5,1024]{3,1,2,0:T(2,128)(2,1)} %copy.118), calls=%async_computation.1 | async-start | bytes 2621440 | tf_op jit(solution)/shard_map/all_to_all | solution.py:74
  287.0 0.3 reduce-scatter.5.cloned.1.call-start
  287.3 2.6 bitcast_convert_fusion.1
  290.2 0.2 reshape.59
  290.4 3.5 gather_fusion
  294.0 0.7 copy.128
  294.7 1.1 reshape.75
  295.8 0.2 copy.134
  296.1 0.8 convert_element_type.93
  296.9 36.7 %reduce-scatter.5.cloned.1.call-done = bf16[2,128,512]{2,1,0:T(8,128)(2,1)} async-done(((bf16[2,1024,512]{2,1,0:T(8,128)(2,1)}), bf16[2,128,512]{2,1,0:T(8,128)(2,1)}) %reduce-scatter.5.cloned.1.call-update) | async-done | bytes 262160 | tf_op jit(solution)/shard_map/reduce_scatter | solution.py:66
  333.6 1.8 convert_element_type.91
  335.4 0.5 copy.124
  336.0 0.6 reshape.58
  336.6 1.1 convolution_convert_fusion.1
  337.7 10.6 %all-to-all-done.1 = bf16[64,2,5,1024]{3,1,2,0:T(2,128)(2,1)} async-done(((bf16[64,2,5,1024]{3,1,2,0:T(2,128)(2,1)}), bf16[64,2,5,1024]{3,1,2,0:T(2,128)(2,1)}, u32[]{:S(2)}, u32[]{:S(2)}) %all-to-all-start.1) | async-done | bytes 1310752 | tf_op jit(solution)/shard_map/all_to_all | solution.py:74
  348.3 1.8 copy.119
  350.2 0.6 reshape.56
  350.8 2.0 convolution_convert_fusion.2
  (52 shorter events, 1.7 us)
Async XLA Ops:
  7.2 1.9 copy-start.10
  7.2 2.0 copy-start.11
  7.2 23.3 %copy-start.8 = (bf16[128,1024]{1,0:T(8,128)(2,1)S(1)}, bf16[128,1024]{1,0:T(8,128)(2,1)}, u32[]{:S(2)}) copy-start(bf16[128,1024]{1,0:T(8,128)(2,1)} %param.11) | copy-start | bytes 786436
  7.2 23.3 %copy-start.9 = (bf16[128,1024]{1,0:T(8,128)(2,1)S(1)}, bf16[128,1024]{1,0:T(8,128)(2,1)}, u32[]{:S(2)}) copy-start(bf16[128,1024]{1,0:T(8,128)(2,1)} %param.6) | copy-start | bytes 786436
  9.3 0.7 copy-start.2
  11.0 32.7 %all-to-all-start.2 = ((bf16[64,2,5]{2,1,0:T(2,128)(2,1)}), bf16[64,2,5]{2,1,0:T(2,128)(2,1)S(1)}, u32[]{:S(2)}, u32[]{:S(2)}) async-start(bf16[64,2,5]{2,1,0:T(2,128)(2,1)} %reshape.57), calls=%async_computation.2 | async-start | bytes 65536 | tf_op jit(solution)/shard_map/all_to_all | solution.py:38
  43.7 128.0 %all-to-all-start = ((bf16[64,2,5,2048]{3,1,2,0:T(2,128)(2,1)}), bf16[64,2,5,2048]{3,1,2,0:T(2,128)(2,1)S(1)}, u32[]{:S(2)}, u32[]{:S(2)}) async-start(bf16[64,2,5,2048]{3,1,2,0:T(2,128)(2,1)} %copy.116), calls=%async_computation | async-start | bytes 5242880 | tf_op jit(solution)/shard_map/all_to_all | solution.py:37
  55.6 119.4 %all-gather.3.cloned.1.call-start = ((), (), s32[]{:S(2)}) async-start(), calls=%async_computation.7 | async-start | bytes 2359296 | tf_op jit(solution)/shard_map/all_gather | solution.py:46
  56.3 121.6 %all-gather.5.cloned.1.call-start = ((), (), s32[]{:S(2)}) async-start(), calls=%async_computation.8 | async-start | bytes 2359296 | tf_op jit(solution)/shard_map/all_gather | solution.py:47
  175.0 3.0 copy-start.3
  177.9 16.9 %copy-start.4 = (f32[64,2,5,512]{3,0,2,1:T(8,128)}, f32[64,2,5,512]{3,0,2,1:T(8,128)S(1)}, u32[]{:S(2)}) copy-start(f32[64,2,5,512]{3,0,2,1:T(8,128)S(1)} %fusion.19) | copy-start | bytes 3932164
  183.0 25.1 %all-to-all-start.4 = ((bf16[64,2,5]{2,1,0:T(2,128)(2,1)}), bf16[64,2,5]{2,1,0:T(2,128)(2,1)S(1)}, u32[]{:S(2)}, u32[]{:S(2)}) async-start(bf16[64,2,5]{2,1,0:T(2,128)(2,1)} %copy.126), calls=%async_computation.4 | async-start | bytes 65536 | tf_op jit(solution)/shard_map/all_to_all | solution.py:75
  194.8 3.6 %copy-start = (bf16[2,1024,512]{2,1,0:T(8,128)(2,1)S(1)}, bf16[2,1024,512]{2,1,0:T(8,128)(2,1)}, u32[]{:S(2)}) copy-start(bf16[2,1024,512]{2,1,0:T(8,128)(2,1)} %all-gather.3.cloned.1.call-done) | copy-start | bytes 6291460
  198.4 0.9 copy-start.6
  208.2 69.5 %all-to-all-start.3 = ((bf16[64,2,5,1024]{3,1,2,0:T(2,128)(2,1)}), bf16[64,2,5,1024]{3,1,2,0:T(2,128)(2,1)S(1)}, u32[]{:S(2)}, u32[]{:S(2)}) async-start(bf16[64,2,5,1024]{3,1,2,0:T(2,128)(2,1)} %copy.123), calls=%async_computation.3 | async-start | bytes 2621440 | tf_op jit(solution)/shard_map/all_to_all | solution.py:76
  216.3 78.4 %reduce-scatter.7.cloned.1.call-start = ((), (), s32[]{:S(2)}) async-start(), calls=%async_computation.10 | async-start | bytes 2359296
  227.3 1.3 copy-start.5
  231.0 56.2 %copy-start.1 = (bf16[64,2,5,1024]{3,1,2,0:T(2,128)(2,1)S(1)}, bf16[64,2,5,1024]{3,1,2,0:T(2,128)(2,1)}, u32[]{:S(2)}) copy-start(bf16[64,2,5,1024]{3,1,2,0:T(2,128)(2,1)} %get-tuple-element.43) | copy-start | bytes 3932164
  231.0 56.2 %copy-start.7 = (bf16[64,2,5,512]{3,0,2,1:T(8,128)(2,1)S(1)}, bf16[64,2,5,512]{3,0,2,1:T(8,128)(2,1)}, u32[]{:S(2)}) copy-start(bf16[64,2,5,512]{3,0,2,1:T(8,128)(2,1)} %copy-done.6) | copy-start | bytes 1966084
  277.7 70.7 %all-to-all-start.1 = ((bf16[64,2,5,1024]{3,1,2,0:T(2,128)(2,1)}), bf16[64,2,5,1024]{3,1,2,0:T(2,128)(2,1)}, u32[]{:S(2)}, u32[]{:S(2)}) async-start(bf16[64,2,5,1024]{3,1,2,0:T(2,128)(2,1)} %copy.118), calls=%async_computation.1 | async-start | bytes 2621440 | tf_op jit(solution)/shard_map/all_to_all | solution.py:74
  287.0 46.7 %reduce-scatter.5.cloned.1.call-start = ((), (), s32[]{:S(2)}) async-start(), calls=%async_computation.9 | async-start | bytes 2359296 | tf_op jit(solution)/shard_map/reduce_scatter | solution.py:66
Sparse Core Ops, SparseCore 0:
  58.6 34.8 all-gather.2
  95.6 35.2 all-gather.4
  227.4 42.5 reduce-scatter.6
  290.3 43.2 reduce-scatter.4
where the time goes:
time: 365 us; the launch traced here: 359 us
  waiting for transfers between devices  219 us (60%)
  starting transfers between devices  60.8 us (17%)
  local copies, waits for them, and re-layouts  39.3 us (11%)
  matrix products  22.6 us (6%)
  between operations  14.1 us (4%)
    all_to_all x1, waiting for transfers between devices, shards(): lax.all_to_all(packed, 'expert', split_axis=0, concat_axis=0, tiled=True)  114 us
    all_to_all x1, waiting for transfers between devices, shards(): lax.all_to_all(row_grad, 'expert', split_axis=0, concat_axis=0, tiled=True)  46.6 us
    reduce_scatter x1, waiting for transfers between devices, shards(): lax.psum_scatter(part_up.astype(jnp.bfloat16), 'dp', scatter_dimension=1,...  36.7 us
    all_to_all x1, starting transfers between devices, shards(): lax.all_to_all(slot_gate, 'expert', split_axis=0, concat_axis=0, tiled=True)  19.3 us
    all_to_all x1, starting transfers between devices, shards(): lax.all_to_all(packed, 'expert', split_axis=0, concat_axis=0, tiled=True)  11.9 us
    all_to_all x1, starting transfers between devices, shards(): lax.all_to_all(slot_dot, 'expert', split_axis=0, concat_axis=0, tiled=True)  11.7 us
    unnamed x31, local copies, waits for them, and re-layouts  11.6 us
    all_to_all x1, waiting for transfers between devices, shards(): lax.all_to_all(outs, 'expert', split_axis=0, concat_axis=0, tiled=True)  10.6 us
  transfers between devices with their start and end apart: 9, of which 6 were waited for; matrix products, arithmetic and copies ran while one was open for 14% of the time, Pallas kernels for 0%

commit v1 on v0

v1 whole, which is shorter than its diff:
```python
import jax
import jax.numpy as jnp
from jax import lax
from jax.experimental import pallas as pl
from jax.experimental.pallas import tpu as pltpu
from jax.sharding import PartitionSpec as P

NX, NY, NZ = 4, 4, 16
TOK, D, FF, TOP = 128, 1024, 512, 4
BF = jnp.bfloat16
F32 = jnp.float32
MESH_ID = pl.DeviceIdType.MESH
ANY = pl.BlockSpec(memory_space=pl.ANY)
VM = pl.BlockSpec(memory_space=pltpu.VMEM)


def slot_r(k):
    return 15 if k == 8 else 2 * k - 1


def slot_l(k):
    return 15 if k == 8 else 2 * k


def places():
    dp, ex = lax.axis_index("dp"), lax.axis_index("expert")
    x, c = lax.div(dp, 2), lax.rem(dp, 2)
    z, y = lax.div(ex, NY), lax.rem(ex, NY)
    right = (dp, lax.rem(z + 1, NZ) * NY + y)
    left = (dp, lax.rem(z + NZ - 1, NZ) * NY + y)
    sib = (x * 2 + 1 - c, ex)
    xs = [(lax.rem(x + i, NX) * 2 + c, ex) for i in range(1, NX)]
    ys = [(dp, z * NY + lax.rem(y + i, NY)) for i in range(1, NY)]
    return x, y, z, c, right, left, sib, xs, ys


def greet(partners):
    barrier = pltpu.get_barrier_semaphore()
    for p in partners:
        pl.semaphore_signal(barrier, inc=1, device_id=p, device_id_type=MESH_ID)
    pl.semaphore_wait(barrier, len(partners))


def remote(src, dst, send, recv, to):
    return pltpu.make_async_remote_copy(
        src_ref=src, dst_ref=dst, send_sem=send, recv_sem=recv, device_id=to, device_id_type=MESH_ID
    )


def ag_kernel(tok, cot, meta, wu, wd, T, M, WU, WD, zs, zr, ms, mr, cs, cr, cms, cmr, ws, wr, loc):
    x, y, z, c, right, left, sib, xs, ys = places()
    greet([right, left, sib] + xs + ys)
    own = (tok, cot)
    steps = {}

    def zsend(d, k, h):
        slot = slot_r if d == 0 else slot_l
        src = own[h] if k == 1 else T.at[0, slot(k - 1), h]
        r = remote(src, T.at[0, slot(k), h], zs.at[d, k - 1, h], zr.at[d, k - 1, h], right if d == 0 else left)
        r.start()
        steps[d, k, h] = r

    def msend(d, k):
        slot = slot_r if d == 0 else slot_l
        src = meta if k == 1 else M.at[0, slot(k - 1)]
        r = remote(src, M.at[0, slot(k)], ms.at[d, k - 1], mr.at[d, k - 1], right if d == 0 else left)
        r.start()
        steps[d, k, 2] = r

    for h in (0, 1):
        for d in (0, 1):
            zsend(d, 1, h)
    for d in (0, 1):
        msend(d, 1)
    rows1 = pl.ds(pl.multiple_of(x * 256 + c * 128, 128), 128)
    rows2 = pl.ds(pl.multiple_of(x * 256, 256), 256)
    wl = [
        pltpu.make_async_copy(wu.at[c], WU.at[y, rows1], loc.at[0]),
        pltpu.make_async_copy(wd.at[c], WD.at[y, :, rows1], loc.at[1]),
    ]
    wc = [
        remote(wu.at[1 - c], WU.at[y, rows1], ws.at[0], wr.at[0], sib),
        remote(wd.at[1 - c], WD.at[y, :, rows1], ws.at[1], wr.at[1], sib),
    ]
    for r in wl + wc:
        r.start()
    own_local = [
        pltpu.make_async_copy(tok, T.at[0, 0, 0], loc.at[2]),
        pltpu.make_async_copy(cot, T.at[0, 0, 1], loc.at[3]),
        pltpu.make_async_copy(meta, M.at[0, 0], loc.at[4]),
    ]
    for r in own_local:
        r.start()
    core = [
        remote(tok, T.at[1, 0, 0], cs.at[9], cr.at[9], sib),
        remote(cot, T.at[1, 0, 1], cs.at[0], cr.at[0], sib),
        remote(meta, M.at[1, 0], cms.at[0], cmr.at[0], sib),
    ]
    for r in core:
        r.start()
    for r in wl:
        r.wait()
    for r in wc:
        r.wait_recv()
    w1 = [remote(WU.at[y, rows2], WU.at[y, rows2], ws.at[2 + i], wr.at[2 + i], xs[i]) for i in range(3)]
    w1 += [remote(WD.at[y, :, rows2], WD.at[y, :, rows2], ws.at[5 + i], wr.at[5 + i], ys[i]) for i in range(3)]
    for r in w1:
        r.start()
    w2 = [remote(WU.at[y], WU.at[y], ws.at[8 + i], wr.at[8 + i], ys[i]) for i in range(3)]
    w2 += [remote(WD.at[:, :, rows2], WD.at[:, :, rows2], ws.at[11 + i], wr.at[11 + i], xs[i]) for i in range(3)]

    for k in range(1, 9):
        for h in (0, 1):
            for d in (0, 1):
                if (d, k, h) not in steps:
                    continue
                steps[d, k, h].wait_recv()
                if k < 7 or (k == 7 and h == d):
                    zsend(d, k + 1, h)
        for d in (0, 1):
            if (d, k, 2) not in steps:
                continue
            steps[d, k, 2].wait_recv()
            if k < 7 or (k == 7 and d == 0):
                msend(d, k + 1)
        many = pl.ds(15, 1) if k == 8 else pl.ds(2 * k - 1, 2)
        pair = [
            remote(T.at[0, many], T.at[1, many], cs.at[k], cr.at[k], sib),
            remote(M.at[0, many], M.at[1, many], cms.at[k], cmr.at[k], sib),
        ]
        for r in pair:
            r.start()
        core += pair
        if k == 2:
            for r in w1:
                r.wait_recv()
            for r in w2:
                r.start()
    for r in own_local:
        r.wait()
    for r in w2 + core:
        r.wait_recv()
    for r in list(steps.values()) + wc + w1 + w2 + core:
        r.wait_send()


def codes(m, base, h):
    m = m.astype(F32)
    ids = m[0:4].astype(jnp.int32) - base
    rank = m[4:8].astype(jnp.int32)
    return jnp.where((ids & 1) == 0, ids * 8 + h * 8 + rank, -1), m[8:12]


def mid_kernel(base_ref, T, M, WU, WD, U, GP, PU, PD, X, C, G, O, R, S):
    i = pl.program_id(0)
    base = base_ref[0]

    def selection(pair):
        hot, weight, eqs = [], [], []
        for h in (0, 1):
            code, gate = codes(M[lax.div(pair, 8), lax.rem(pair, 8) * 2 + h], base, h)
            r = lax.broadcasted_iota(jnp.int32, (64, TOK), 0)
            eq = [r == code[k : k + 1] for k in range(TOP)]
            hot.append(sum(jnp.where(e, 1.0, 0.0) for e in eq))
            weight.append(sum(jnp.where(e, gate[k : k + 1], 0.0) for k, e in enumerate(eq)))
            eqs.append(eq)
        return jnp.concatenate(hot, axis=1), jnp.concatenate(weight, axis=1), eqs

    @pl.when(i < 16)
    def _():
        hot, weight, _ = selection(i)
        hot = hot.astype(BF)
        tok = jnp.dot(hot, T[0, :, 0].reshape(2 * TOK, D), preferred_element_type=F32).astype(BF)
        cot = jnp.dot(hot, T[0, :, 1].reshape(2 * TOK, D), preferred_element_type=F32).astype(BF)
        gate = jnp.broadcast_to(jnp.sum(weight, axis=1, keepdims=True), (64, 128))
        rows = pl.ds(pl.multiple_of(i * 16, 16), 16)
        for e in range(4):
            X[e, rows] = tok[e * 16 : e * 16 + 16]
            C[e, rows] = cot[e * 16 : e * 16 + 16]
            G[e, rows] = gate[e * 16 : e * 16 + 16]

    @pl.when((i >= 16) & (i < 20))
    def _():
        e = i - 16
        x, cot, wu, wd = X[e], C[e], WU[0], WD[0]
        pre = jnp.dot(x, wu, preferred_element_type=F32)
        t = jnp.tanh(0.7978845608 * (pre + 0.044715 * pre * pre * pre))
        act = (0.5 * pre * (1.0 + t)).astype(BF)
        slope = 0.5 * (1.0 + t) + 0.5 * pre * (1.0 - t * t) * (0.7978845608 * (1.0 + 0.134145 * pre * pre))
        outs = jnp.dot(act, wd, preferred_element_type=F32).astype(BF)
        O[e] = outs
        S[e] = jnp.broadcast_to(
            jnp.sum(cot.astype(F32) * outs.astype(F32), axis=1, keepdims=True), (256, 128)
        )
        scaled = (G[e][:, 0:1] * cot.astype(F32)).astype(BF)
        act_grad = lax.dot_general(scaled, wd, (((1,), (1,)), ((), ())), preferred_element_type=F32)
        pre_grad = (act_grad * slope).astype(BF)
        R[e] = lax.dot_general(pre_grad, wu, (((1,), (1,)), ((), ())), preferred_element_type=F32).astype(BF)
        PU[0] = lax.dot_general(x, pre_grad, (((0,), (0,)), ((), ())), preferred_element_type=F32).astype(BF)
        PD[0] = lax.dot_general(act, scaled, (((0,), (0,)), ((), ())), preferred_element_type=F32).astype(BF)

    @pl.when(i >= 20)
    def _():
        pair = i - 20
        hot, weight, eqs = selection(pair)
        rows = pl.ds(pl.multiple_of(pair * 16, 16), 16)
        outs = jnp.concatenate([O[e, rows] for e in range(4)], axis=0)
        grad = jnp.concatenate([R[e, rows] for e in range(4)], axis=0)
        dots = jnp.concatenate([S[e, rows] for e in range(4)], axis=0)
        over = (((0,), (0,)), ((), ()))
        mixed = lax.dot_general(weight.astype(BF), outs, over, preferred_element_type=F32).astype(BF)
        back = lax.dot_general(hot.astype(BF), grad, over, preferred_element_type=F32).astype(BF)
        for h in (0, 1):
            U[0, h, 0] = mixed[h * TOK : (h + 1) * TOK]
            U[0, h, 1] = back[h * TOK : (h + 1) * TOK]
            gp = [jnp.sum(jnp.where(eq, dots, 0.0), axis=0, keepdims=True) for eq in eqs[h]]
            gp = jnp.concatenate(gp + [jnp.zeros((12, TOK), F32)], axis=0)
            GP[lax.div(pair, 8), lax.rem(pair, 8) * 2 + h] = gp.astype(BF)


def rs_kernel(
    U, GP, PU, PD, mixed, back, gate, upg, dng,
    A, C, V, GA, GC, GV, RU, OU, SU, RU2, SU2, RU3, RD, OD, SD, RD2, SD2, RD3,
    zs, zr, ms, mr, cs, cr, cms, cmr, ws, wr, loc,
):
    x, y, z, c, right, left, sib, xs, ys = places()
    greet([right, left, sib] + xs + ys)
    groups = [pl.ds(15, 1)] + [pl.ds(2 * k - 1, 2) for k in range(7, 0, -1)] + [pl.ds(0, 1)]
    core, here = [], []
    for n, g in enumerate(groups):
        core.append(
            (
                remote(U.at[1, g], C.at[g], cs.at[n], cr.at[n], sib),
                remote(GP.at[1, g], GC.at[g], cms.at[n], cmr.at[n], sib),
            )
        )
        here.append(
            (
                pltpu.make_async_copy(U.at[0, g], A.at[g], loc.at[n]),
                pltpu.make_async_copy(GP.at[0, g], GA.at[g], loc.at[9 + n]),
            )
        )
        for r in core[n] + here[n]:
            r.start()
    xcols = [pl.ds(pl.multiple_of(lax.rem(x + i, NX) * 256, 256), 256) for i in range(NX)]
    yat = [lax.rem(y + i, NY) for i in range(NY)]
    w1 = [remote(PU.at[yat[i + 1]], RU.at[i], ws.at[i], wr.at[i], ys[i]) for i in range(3)]
    w1 += [remote(PD.at[:, :, xcols[i + 1]], RD.at[i], ws.at[3 + i], wr.at[3 + i], xs[i]) for i in range(3)]
    wl = [
        pltpu.make_async_copy(PU.at[y], OU, loc.at[18]),
        pltpu.make_async_copy(PD.at[:, :, xcols[0]], OD, loc.at[19]),
    ]
    for r in w1 + wl:
        r.start()

    sends = []
    gots = {}

    def zsend(d, k, h):
        slot = (slot_r if d == 0 else slot_l)(k)
        r = remote(A.at[slot, h], V.at[d, k - 1, h], zs.at[d, k - 1, h], zr.at[d, k - 1, h], left if d == 0 else right)
        r.start()
        sends.append(r)
        gots[d, k - 1, h] = r

    def msend(d, k):
        slot = (slot_r if d == 0 else slot_l)(k)
        r = remote(GA.at[slot], GV.at[d, k - 1], ms.at[d, k - 1], mr.at[d, k - 1], left if d == 0 else right)
        r.start()
        sends.append(r)
        gots[d, k - 1, 2] = r

    def add(slot, h, more, dst):
        @pl.loop(0, TOK, step=32)
        def _(at):
            rows = pl.ds(pl.multiple_of(at, 32), 32)
            total = A[slot, h, rows].astype(F32) + C[slot, h, rows].astype(F32)
            for d, k in more:
                total += V[d, k, h, rows].astype(F32)
            dst[rows] = total.astype(BF)

    def add_gate(slot, more):
        total = GA[slot].astype(F32) + GC[slot].astype(F32)
        for d, k in more:
            total += GV[d, k].astype(F32)
        return total.astype(BF)

    for n, k in enumerate(range(8, 0, -1)):
        for r in here[n]:
            r.wait()
        for r in core[n]:
            r.wait_recv()
        order = [(0, 1), (1, 0), (0, 0), (1, 1)] if k == 7 else [(0, 0), (1, 1)] if k == 8 else [(0, 0), (1, 0), (0, 1), (1, 1)]
        for d, h in order:
            slot = (slot_r if d == 0 else slot_l)(k)
            more = []
            if (d, k, h) in gots:
                gots[d, k, h].wait_recv()
                more = [(d, k)]
            add(slot, h, more, A.at[slot, h])
            zsend(d, k, h)
        for d in (0, 1) if k < 8 else (0,):
            slot = (slot_r if d == 0 else slot_l)(k)
            more = []
            if (d, k, 2) in gots:
                gots[d, k, 2].wait_recv()
                more = [(d, k)]
            GA[slot] = add_gate(slot, more)
            msend(d, k)
        if k == 4:
            for r in wl:
                r.wait()
            for r in w1:
                r.wait_recv()

            @pl.loop(0, D, step=32)
            def _(at):
                rows = pl.ds(pl.multiple_of(at, 32), 32)
                total = OU[rows].astype(F32)
                for i in range(3):
                    total += RU[i, rows].astype(F32)
                SU[rows] = total.astype(BF)

            @pl.loop(0, NY)
            def _(j):
                @pl.loop(0, FF, step=64)
                def _(at):
                    rows = pl.ds(pl.multiple_of(at, 64), 64)
                    total = OD[j, rows].astype(F32)
                    for i in range(3):
                        total += RD[i, j, rows].astype(F32)
                    SD[j, rows] = total.astype(BF)

            w2 = [remote(SU.at[xcols[i + 1]], RU2.at[i], ws.at[6 + i], wr.at[6 + i], xs[i]) for i in range(3)]
            w2 += [remote(SD.at[yat[i + 1]], RD2.at[i], ws.at[9 + i], wr.at[9 + i], ys[i]) for i in range(3)]
            for r in w2:
                r.start()
        if k == 2:
            for r in w2:
                r.wait_recv()

            @pl.loop(0, 256, step=32)
            def _(at):
                rows = pl.ds(pl.multiple_of(at, 32), 32)
                total = SU[pl.ds(pl.multiple_of(x * 256 + at, 32), 32)].astype(F32)
                for i in range(3):
                    total += RU2[i, rows].astype(F32)
                SU2[rows] = total.astype(BF)

            @pl.loop(0, FF, step=64)
            def _(at):
                rows = pl.ds(pl.multiple_of(at, 64), 64)
                total = SD[y, rows].astype(F32)
                for i in range(3):
                    total += RD2[i, rows].astype(F32)
                SD2[rows] = total.astype(BF)

            theirs = pl.ds(pl.multiple_of((1 - c) * 128, 128), 128)
            w3 = [
                remote(SU2.at[theirs], RU3, ws.at[12], wr.at[12], sib),
                remote(SD2.at[:, theirs], RD3, ws.at[13], wr.at[13], sib),
            ]
            for r in w3:
                r.start()
    for r in here[8]:
        r.wait()
    for r in core[8]:
        r.wait_recv()
    for r in w3:
        r.wait_recv()
    mine = pl.ds(pl.multiple_of(c * 128, 128), 128)
    upg[c] = SU2[mine].astype(F32)
    upg[1 - c] = RU3[...].astype(F32)
    dng[c] = SD2[:, mine].astype(F32)
    dng[1 - c] = RD3[...].astype(F32)
    for h, dst in ((0, mixed), (1, back)):
        for d in (0, 1):
            gots[d, 0, h].wait_recv()
        add(0, h, [(0, 0), (1, 0)], dst)
    for d in (0, 1):
        gots[d, 0, 2].wait_recv()
    gate[...] = add_gate(0, [(0, 0), (1, 0)])
    for r in sends + w1 + w2 + w3 + [r for pair in core for r in pair]:
        r.wait_send()


def shards(tokens, expert_ids, gates, w_up, w_down, out_grad):
    dma = pltpu.SemaphoreType.DMA
    z, c = lax.axis_index("expert") // NY, lax.axis_index("dp") % 2
    experts = NZ * NY * 2
    hot = (expert_ids[:, :, None] == jnp.arange(experts, dtype=jnp.int32)).astype(F32)
    before = jnp.dot(jnp.tri(TOK, k=-1, dtype=BF), jnp.sum(hot, axis=1).astype(BF), preferred_element_type=F32)
    ranks = jnp.sum(before[:, None, :] * hot, axis=2)
    meta = jnp.concatenate(
        [expert_ids.astype(BF).T, ranks.astype(BF).T, gates.T, jnp.zeros((4, TOK), BF)], axis=0
    )
    sd = jax.ShapeDtypeStruct
    T, M, WU, WD = pl.pallas_call(
        ag_kernel,
        name="gather",
        out_shape=(
            sd((2, NZ, 2, TOK, D), BF),
            sd((2, NZ, 16, TOK), BF),
            sd((NY, D, FF), BF),
            sd((NY, FF, D), BF),
        ),
        in_specs=[ANY] * 5,
        out_specs=[ANY] * 4,
        scratch_shapes=[dma((2, 8, 2))] * 2 + [dma((2, 8))] * 2 + [dma((10,))] * 2 + [dma((9,))] * 2 + [dma((14,))] * 2 + [dma((5,))],
        compiler_params=pltpu.CompilerParams(collective_id=1, has_side_effects=True),
    )(tokens, out_grad, meta, w_up, w_down)

    base = (z * (2 * NY) + c).astype(jnp.int32).reshape(1)
    pack = lambda i: jnp.minimum(i, 15)
    expert = lambda i: jnp.clip(i - 16, 0, 3)
    unpack = lambda i: jnp.maximum(i - 20, 0)
    U, GP, PU, PD = pl.pallas_call(
        mid_kernel,
        name="experts",
        grid=(36,),
        out_shape=(
            sd((2, NZ, 2, TOK, D), BF),
            sd((2, NZ, 16, TOK), BF),
            sd((NY, D, FF), BF),
            sd((NY, FF, D), BF),
        ),
        in_specs=[
            pl.BlockSpec(memory_space=pltpu.SMEM),
            pl.BlockSpec((1, 2, 2, TOK, D), lambda i: (pack(i) // 8, pack(i) % 8, 0, 0, 0)),
            pl.BlockSpec((2, NZ, 16, TOK), lambda i: (0, 0, 0, 0)),
            pl.BlockSpec((1, D, FF), lambda i: (expert(i), 0, 0)),
            pl.BlockSpec((1, FF, D), lambda i: (expert(i), 0, 0)),
        ],
        out_specs=[
            pl.BlockSpec((1, 2, 2, TOK, D), lambda i: (unpack(i) // 8, unpack(i) % 8, 0, 0, 0)),
            pl.BlockSpec((2, NZ, 16, TOK), lambda i: (0, 0, 0, 0)),
            pl.BlockSpec((1, D, FF), lambda i: (expert(i), 0, 0)),
            pl.BlockSpec((1, FF, D), lambda i: (expert(i), 0, 0)),
        ],
        scratch_shapes=[
            pltpu.VMEM((4, 256, D), BF),
            pltpu.VMEM((4, 256, D), BF),
            pltpu.VMEM((4, 256, 128), F32),
            pltpu.VMEM((4, 256, D), BF),
            pltpu.VMEM((4, 256, D), BF),
            pltpu.VMEM((4, 256, 128), F32),
        ],
        compiler_params=pltpu.CompilerParams(vmem_limit_bytes=50 << 20, dimension_semantics=("arbitrary",)),
    )(base, T, M, WU, WD)

    vm = pltpu.VMEM
    mixed, back, gate, upg, dng = pl.pallas_call(
        rs_kernel,
        name="scatter",
        out_shape=(
            sd((TOK, D), BF),
            sd((TOK, D), BF),
            sd((16, TOK), BF),
            sd((2, D // 8, FF), F32),
            sd((2, FF, D // 8), F32),
        ),
        in_specs=[ANY] * 4,
        out_specs=[VM] * 5,
        scratch_shapes=[
            vm((NZ, 2, TOK, D), BF), vm((NZ, 2, TOK, D), BF), vm((2, 8, 2, TOK, D), BF),
            vm((NZ, 16, TOK), BF), vm((NZ, 16, TOK), BF), vm((2, 8, 16, TOK), BF),
            vm((3, D, FF), BF), vm((D, FF), BF), vm((D, FF), BF), vm((3, 256, FF), BF), vm((256, FF), BF), vm((128, FF), BF),
            vm((3, NY, FF, 256), BF), vm((NY, FF, 256), BF), vm((NY, FF, 256), BF), vm((3, FF, 256), BF), vm((FF, 256), BF), vm((FF, 128), BF),
        ] + [dma((2, 8, 2))] * 2 + [dma((2, 8))] * 2 + [dma((9,))] * 4 + [dma((14,))] * 2 + [dma((20,))],
        compiler_params=pltpu.CompilerParams(collective_id=2, has_side_effects=True, vmem_limit_bytes=56 << 20),
    )(U, GP, PU, PD)
    return mixed, back, gate[:TOP].T, upg, dng


def solution(mesh):
    rows = P(("dp", "expert"), None)
    up, down = P("expert", "dp", None), P("expert", None, "dp")
    return jax.shard_map(
        shards,
        mesh=mesh,
        in_specs=(rows, rows, rows, up, down, rows),
        out_specs=(rows, rows, rows, up, down),
        check_vma=False,
    )
```

time: 365 us -> 254 us (0.70); the launches traced: 359 us -> 253 us
  Pallas kernels: 0 us -> 238 us
  waiting for transfers between devices: 219 us -> 0 us
  starting transfers between devices: 60.8 us -> 0 us
  local copies, waits for them, and re-layouts: 39.3 us -> 9.94 us
  matrix products: 22.6 us -> 0.2 us
  between operations: 14.1 us -> 0.7 us
    pallas_call x0 -> x3, Pallas kernels: none -> 238 us  [the longest x1 104 us: shards(): pl.pallas_call(ag_kernel, name='gather', out_shape=(sd((2, NZ, 2, TOK, D)...]
    all_to_all x5 -> x0, waiting for transfers between devices: 181 us -> none  [the longest x1 114 us: shards(): lax.all_to_all(packed, 'expert', split_axis=0, concat_axis=0, tiled=True)]
    all_to_all x5 -> x0, starting transfers between devices: 60.4 us -> none  [the longest x1 19.3 us: shards(): lax.all_to_all(slot_gate, 'expert', split_axis=0, concat_axis=0, tiled=True)]
    reduce_scatter x1 -> x0, waiting for transfers between devices: 36.7 us -> none  [shards(): lax.psum_scatter(part_up.astype(jnp.bfloat16), 'dp', scatter_dimension=1,...]
    dot_general x9 -> x1, matrix products: 22.6 us -> 0.2 us  [shards(): jnp.dot(jnp.tri(TOK, k=-1, dtype=BF), jnp.sum(hot, axis=1).astype(BF), pr...]
    reshape x6 -> x0, local copies, waits for them, and re-layouts: 12 us -> none  [the longest x2 9.75 us: shards(): packed = packed.reshape(peers, local, capacity, 2 * width)]
    convert_element_type x4 -> x0, local copies, waits for them, and re-layouts: 5.57 us -> none  [the longest x1 2.42 us: shards(): outs = jnp.einsum('secf,efd->secd', act_b, full_down, preferred_element_t...]
    unnamed x31 -> x8, local copies, waits for them, and re-layouts: 11.6 us -> 8.62 us
  transfers between devices with their start and end apart: 9 -> 0, of which waited for: 6 -> 0; matrix products, arithmetic and copies ran while one was open for 14% -> 0% of each run, Pallas kernels for 0% -> 0%
where the time goes in v1:
time: 254 us; the launch traced here: 253 us
  Pallas kernels  238 us (94%)
  local copies, waits for them, and re-layouts  9.94 us (4%)
  other arithmetic  3.78 us (1%)
    pallas_call x1, Pallas kernels, shards(): pl.pallas_call(ag_kernel, name='gather', out_shape=(sd((2, NZ, 2, TOK, D)...  104 us
    pallas_call x1, Pallas kernels, shards(): pl.pallas_call(rs_kernel, name='scatter', out_shape=(sd((TOK, D), BF), sd...  97.6 us
    pallas_call x1, Pallas kernels, shards(): pl.pallas_call(mid_kernel, name='experts', grid=(36,), out_shape=(sd((2,...  36.8 us
    unnamed x8, local copies, waits for them, and re-layouts  8.62 us

profile of v1, /device:TPU:1, one launch (start us, length us, event | category | flops | bytes accessed | tf_op | source)
XLA Modules:
  0.0 253.1 jit_solution(18332632107043552316)
XLA Ops:
  0.7 0.1 pad.3.clone
  0.7 0.7 convert_bitcast_fusion.1
  1.4 0.8 convert_reduce_fusion
  2.3 0.2 fusion
  2.5 0.9 select_reduce_fusion
  3.4 1.4 maximum_maximum_fusion.meta
  4.7 104.0 %gather.1 = (bf16[2,16,2,128,1024]{4,3,2,1,0:T(8,128)(2,1)}, bf16[2,16,16,128]{3,2,1,0:T(8,128)(2,1)}, bf16[4,1024,512]{2,1,0:T(8,128)(2,1)}, bf16[4,512,1024]{2,1,0:T(8,128)(2,1)}) custom-call(bf16[128,1024]{1,0:T(8,128)(2,1)} %tok.1, bf16[128,1024]{1,0:T(8,128)(2,1)} %cot.1, bf16[16,128]{1,0:T(8,128)(2,1)} %maximum_maximum_fusion.meta, ...), custom_call_target="tpu_custom_call" | custom-call | tf_op jit(solution)/shard_map/gather/pallas_call | solution.py:398
  108.8 0.0 copy-start.1
  108.8 0.9 copy-done.1
  109.7 36.8 %experts.1 = (bf16[2,16,2,128,1024]{4,3,2,1,0:T(8,128)(2,1)}, bf16[2,16,16,128]{3,2,1,0:T(8,128)(2,1)S(1)}, bf16[4,1024,512]{2,1,0:T(8,128)(2,1)}, bf16[4,512,1024]{2,1,0:T(8,128)(2,1)}) custom-call(s32[1]{0:T(128)} %bitcast.base_ref, bf16[2,16,2,128,1024]{4,3,2,1,0:T(8,128)(2,1)} %get-tuple-element.18.T, bf16[2,16,16,128]{3,2,1,0:T(8,128)(2,1)S(1)} %copy-done.1, ...), custom_call_target="tpu_custom_call" | custom-call | tf_op jit(solution)/shard_map/experts/pallas_call | solution.py:417
  146.5 0.0 copy-start
  146.5 0.7 copy-done
  147.1 97.6 %scatter.1 = (bf16[128,1024]{1,0:T(8,128)(2,1)}, bf16[128,1024]{1,0:T(8,128)(2,1)}, bf16[16,128]{1,0:T(8,128)(2,1)}, f32[2,128,512]{2,1,0:T(8,128)}, f32[2,512,128]{2,1,0:T(8,128)}) custom-call(bf16[2,16,2,128,1024]{4,3,2,1,0:T(8,128)(2,1)} %get-tuple-element.22.U, bf16[2,16,16,128]{3,2,1,0:T(8,128)(2,1)} %copy-done, ...), custom_call_target="tpu_custom_call" | custom-call | tf_op jit(solution)/shard_map/scatter/pallas_call | solution.py:452
  244.7 1.2 slice_bitcast_fusion
  246.0 1.7 copy.16
  247.6 1.7 copy.17
  249.3 1.9 copy.18
  251.2 1.9 copy.19
  (2 shorter events, 0.0 us)
Async XLA Ops:
  108.8 0.9 copy-start.1
  146.5 0.7 copy-start

commit v2 on v1

v2 whole, which is shorter than its diff:
```python
import jax
import jax.numpy as jnp
from jax import lax
from jax.experimental import pallas as pl
from jax.experimental.pallas import tpu as pltpu
from jax.sharding import PartitionSpec as P

NX, NY, NZ = 4, 4, 16
TOK, D, FF, TOP = 128, 1024, 512, 4
BF = jnp.bfloat16
F32 = jnp.float32
MESH_ID = pl.DeviceIdType.MESH
ANY = pl.BlockSpec(memory_space=pl.ANY)
VM = pl.BlockSpec(memory_space=pltpu.VMEM)


def slot_r(k):
    return 15 if k == 8 else 2 * k - 1


def slot_l(k):
    return 15 if k == 8 else 2 * k


def places():
    dp, ex = lax.axis_index("dp"), lax.axis_index("expert")
    x, c = lax.div(dp, 2), lax.rem(dp, 2)
    z, y = lax.div(ex, NY), lax.rem(ex, NY)
    right = (dp, lax.rem(z + 1, NZ) * NY + y)
    left = (dp, lax.rem(z + NZ - 1, NZ) * NY + y)
    sib = (x * 2 + 1 - c, ex)
    xs = [(lax.rem(x + i, NX) * 2 + c, ex) for i in range(1, NX)]
    ys = [(dp, z * NY + lax.rem(y + i, NY)) for i in range(1, NY)]
    return x, y, z, c, right, left, sib, xs, ys


def greet(partners):
    barrier = pltpu.get_barrier_semaphore()
    for p in partners:
        pl.semaphore_signal(barrier, inc=1, device_id=p, device_id_type=MESH_ID)
    pl.semaphore_wait(barrier, len(partners))


def remote(src, dst, send, recv, to):
    return pltpu.make_async_remote_copy(
        src_ref=src, dst_ref=dst, send_sem=send, recv_sem=recv, device_id=to, device_id_type=MESH_ID
    )


def selection(meta_a, meta_b, first, core):
    hot, weight, eqs = [], [], []
    for h, m in enumerate((meta_a, meta_b)):
        m = m.astype(F32)
        at = m[0:4].astype(jnp.int32) - first
        rank = m[4:8].astype(jnp.int32)
        row = jnp.where((at & 1) == core, 0, 64) + (at >> 1) * 16 + h * 8 + rank
        row = jnp.where((at >= 0) & (at < 8), row, -1)
        r = lax.broadcasted_iota(jnp.int32, (128, TOK), 0)
        eq = [r == row[k : k + 1] for k in range(TOP)]
        hot.append(sum(jnp.where(e, 1.0, 0.0) for e in eq))
        weight.append(sum(jnp.where(e, m[8 + k : 9 + k], 0.0) for k, e in enumerate(eq)))
        eqs.append(eq)
    return jnp.concatenate(hot, axis=1), jnp.concatenate(weight, axis=1), eqs


def pair_slots(p):
    return (0, 15) if p == 0 else (2 * p - 1, 2 * p)


def ag_kernel(
    tok, cot, ids, gates, wu, wd, X, MO, WU, WD,
    T, M, B, zs, zr, ms, mr, ps, pr, lp, ws, wr, loc,
):
    x, y, z, c, right, left, sib, xs, ys = places()
    greet([right, left, sib] + xs + ys)
    own = (tok, cot)
    steps = {}

    def zsend(d, k, h):
        slot = slot_r if d == 0 else slot_l
        src = own[h] if k == 1 else T.at[slot(k - 1), h]
        r = remote(src, T.at[slot(k), h], zs.at[d, k - 1, h], zr.at[d, k - 1, h], right if d == 0 else left)
        r.start()
        steps[d, k, h] = r

    def msend(d, k):
        slot = slot_r if d == 0 else slot_l
        src = M.at[0 if k == 1 else slot(k - 1)]
        r = remote(src, M.at[slot(k)], ms.at[d, k - 1], mr.at[d, k - 1], right if d == 0 else left)
        r.start()
        steps[d, k, 2] = r

    for h in (0, 1):
        for d in (0, 1):
            zsend(d, 1, h)
    rows1 = pl.ds(pl.multiple_of(x * 256 + c * 128, 128), 128)
    rows2 = pl.ds(pl.multiple_of(x * 256, 256), 256)
    wl = [
        pltpu.make_async_copy(wu.at[c], WU.at[y, rows1], loc.at[0]),
        pltpu.make_async_copy(wd.at[c], WD.at[y, :, rows1], loc.at[1]),
    ]
    wc = [
        remote(wu.at[1 - c], WU.at[y, rows1], ws.at[0], wr.at[0], sib),
        remote(wd.at[1 - c], WD.at[y, :, rows1], ws.at[1], wr.at[1], sib),
    ]
    own_local = [
        pltpu.make_async_copy(tok, T.at[0, 0], loc.at[2]),
        pltpu.make_async_copy(cot, T.at[0, 1], loc.at[3]),
    ]
    for r in wl + wc + own_local:
        r.start()
    e = lax.broadcasted_iota(jnp.int32, (128, TOK), 0)
    eq = [e == ids[k : k + 1] for k in range(TOP)]
    hot = sum(jnp.where(q, 1.0, 0.0) for q in eq)
    earlier = jnp.where(e < lax.broadcasted_iota(jnp.int32, (128, TOK), 1), 1.0, 0.0)
    before = jnp.dot(hot.astype(BF), earlier.astype(BF), preferred_element_type=F32)
    ranks = [jnp.sum(jnp.where(q, before, 0.0), axis=0, keepdims=True) for q in eq]
    M[0] = jnp.concatenate(
        [ids[...].astype(F32)] + ranks + [gates[...].astype(F32), jnp.zeros((4, TOK), F32)], axis=0
    ).astype(BF)
    for d in (0, 1):
        msend(d, 1)
    for r in wl:
        r.wait()
    for r in wc:
        r.wait_recv()
    w1 = [remote(WU.at[y, rows2], WU.at[y, rows2], ws.at[2 + i], wr.at[2 + i], xs[i]) for i in range(3)]
    w1 += [remote(WD.at[y, :, rows2], WD.at[y, :, rows2], ws.at[5 + i], wr.at[5 + i], ys[i]) for i in range(3)]
    for r in w1:
        r.start()
    w2 = [remote(WU.at[y], WU.at[y], ws.at[8 + i], wr.at[8 + i], ys[i]) for i in range(3)]
    w2 += [remote(WD.at[:, :, rows2], WD.at[:, :, rows2], ws.at[11 + i], wr.at[11 + i], xs[i]) for i in range(3)]

    packed = []

    def pack(p):
        a, b = pair_slots(p)
        hot, weight, _ = selection(M[a], M[b], z * 8, c)
        hot = hot.astype(BF)
        gate = jnp.sum(weight, axis=1, keepdims=True)
        t = jnp.dot(hot, jnp.concatenate([T[a, 0], T[b, 0]], axis=0), preferred_element_type=F32)
        g = jnp.dot(hot, jnp.concatenate([T[a, 1], T[b, 1]], axis=0), preferred_element_type=F32)
        for n, v in enumerate((t.astype(BF), g.astype(BF), (g * gate).astype(BF))):
            for q in range(8):
                B[p, q // 4, n, q % 4] = v[q * 16 : q * 16 + 16]
        here = pltpu.make_async_copy(B.at[p, 0], X.at[:, :, pl.ds(p * 16, 16)], lp.at[p])
        there = remote(B.at[p, 1], X.at[:, :, pl.ds(128 + p * 16, 16)], ps.at[p], pr.at[p], sib)
        here.start()
        there.start()
        packed.append((here, there))

    for k in range(1, 9):
        for h in (0, 1):
            for d in (0, 1):
                if (d, k, h) not in steps:
                    continue
                steps[d, k, h].wait_recv()
                if k < 7 or (k == 7 and h == d):
                    zsend(d, k + 1, h)
        for d in (0, 1):
            if (d, k, 2) not in steps:
                continue
            steps[d, k, 2].wait_recv()
            if k < 7 or (k == 7 and d == 0):
                msend(d, k + 1)
        if k == 1:
            for r in own_local:
                r.wait()
        if k == 2:
            for r in w1:
                r.wait_recv()
            for r in w2:
                r.start()
        pack(k % 8)
    out = pltpu.make_async_copy(M, MO, loc.at[4])
    out.start()
    for r in w2:
        r.wait_recv()
    for here, there in packed:
        here.wait()
        there.wait_recv()
    for r in list(steps.values()) + wc + w1 + w2 + [there for _, there in packed]:
        r.wait_send()
    out.wait()


def mid_kernel(X, WU, WD, O, S, PU, PD):
    x, cot, scaled, wu, wd = X[0, 0], X[1, 0], X[2, 0], WU[0], WD[0]
    pre = jnp.dot(x, wu, preferred_element_type=F32)
    t = jnp.tanh(0.7978845608 * (pre + 0.044715 * pre * pre * pre))
    act = (0.5 * pre * (1.0 + t)).astype(BF)
    slope = 0.5 * (1.0 + t) + 0.5 * pre * (1.0 - t * t) * (0.7978845608 * (1.0 + 0.134145 * pre * pre))
    act_grad = lax.dot_general(scaled, wd, (((1,), (1,)), ((), ())), preferred_element_type=F32)
    pre_grad = (act_grad * slope).astype(BF)
    outs = jnp.dot(act, wd, preferred_element_type=F32).astype(BF)
    O[0, 0] = outs
    S[0] = jnp.broadcast_to(jnp.sum(cot.astype(F32) * outs.astype(F32), axis=1, keepdims=True), (256, 128))
    O[1, 0] = lax.dot_general(pre_grad, wu, (((1,), (1,)), ((), ())), preferred_element_type=F32).astype(BF)
    PU[0] = lax.dot_general(x, pre_grad, (((0,), (0,)), ((), ())), preferred_element_type=F32).astype(BF)
    PD[0] = lax.dot_general(act, scaled, (((0,), (0,)), ((), ())), preferred_element_type=F32).astype(BF)


def rs_kernel(
    O, S, MI, PU, PD, F, GO, UG, DG,
    OL, SL, M, A, V, GA, GV, FV, GF, RU, OU, SU, RU2, SU2, RU3, RD, OD, SD, RD2, SD2, RD3,
    zs, zr, ms, mr, cs, cr, ws, wr, loc,
):
    x, y, z, c, right, left, sib, xs, ys = places()
    greet([right, left, sib] + xs + ys)
    parts = [(0, 16), (112, 16), (16, 96)]
    core, here = [], [pltpu.make_async_copy(MI, M, loc.at[0])]
    here[0].start()
    for n, (at, size) in enumerate(parts):
        a, b = pl.ds(at, size), pl.ds(128 + at, size)
        pair = [
            remote(O.at[:, :, b], OL.at[1, :, :, a], cs.at[n], cr.at[n], sib),
            remote(S.at[:, b], SL.at[1, :, a], cs.at[3 + n], cr.at[3 + n], sib),
        ]
        mine = [
            pltpu.make_async_copy(O.at[:, :, a], OL.at[0, :, :, a], loc.at[1 + n]),
            pltpu.make_async_copy(S.at[:, a], SL.at[0, :, a], loc.at[4 + n]),
        ]
        for r in pair + mine:
            r.start()
        core.append(pair)
        here += mine
    xcols = [pl.ds(pl.multiple_of(lax.rem(x + i, NX) * 256, 256), 256) for i in range(NX)]
    yat = [lax.rem(y + i, NY) for i in range(NY)]
    w1 = [remote(PU.at[yat[i + 1]], RU.at[i], ws.at[i], wr.at[i], ys[i]) for i in range(3)]
    w1 += [remote(PD.at[:, :, xcols[i + 1]], RD.at[i], ws.at[3 + i], wr.at[3 + i], xs[i]) for i in range(3)]
    wl = [
        pltpu.make_async_copy(PU.at[y], OU, loc.at[7]),
        pltpu.make_async_copy(PD.at[:, :, xcols[0]], OD, loc.at[8]),
    ]
    for r in w1 + wl:
        r.start()

    sends = []
    gots = {}

    def zsend(d, k, h):
        slot = (slot_r if d == 0 else slot_l)(k)
        r = remote(A.at[slot, h], V.at[d, k - 1, h], zs.at[d, k - 1, h], zr.at[d, k - 1, h], left if d == 0 else right)
        r.start()
        sends.append(r)
        gots[d, k - 1, h] = r

    def msend(d, k):
        slot = (slot_r if d == 0 else slot_l)(k)
        r = remote(GA.at[slot], GV.at[d, k - 1], ms.at[d, k - 1], mr.at[d, k - 1], left if d == 0 else right)
        r.start()
        sends.append(r)
        gots[d, k - 1, 2] = r

    def add(slot, h, more, dst):
        @pl.loop(0, TOK, step=32)
        def _(at):
            rows = pl.ds(pl.multiple_of(at, 32), 32)
            total = A[slot, h, rows].astype(F32)
            for d, k in more:
                total += V[d, k, h, rows].astype(F32)
            dst[rows] = total.astype(BF)

    def add_gate(slot, more):
        total = GA[slot].astype(F32)
        for d, k in more:
            total += GV[d, k].astype(F32)
        return total.astype(BF)

    def unpack(p):
        slots = pair_slots(p)
        hot, weight, eqs = selection(M[slots[0]], M[slots[1]], z * 8, c)
        rows = pl.ds(p * 16, 16)
        over = (((0,), (0,)), ((), ()))
        for n, w in enumerate((weight, hot)):
            v = jnp.concatenate([OL[q // 4, n, q % 4, rows] for q in range(8)], axis=0)
            u = lax.dot_general(w.astype(BF), v, over, preferred_element_type=F32).astype(BF)
            for h, slot in enumerate(slots):
                A[slot, n] = u[h * TOK : (h + 1) * TOK]
        dots = jnp.concatenate([SL[q // 4, q % 4, rows] for q in range(8)], axis=0)
        for h, slot in enumerate(slots):
            gp = [jnp.sum(jnp.where(eq, dots, 0.0), axis=0, keepdims=True) for eq in eqs[h]]
            GA[slot] = jnp.concatenate(gp + [jnp.zeros((12, TOK), F32)], axis=0).astype(BF)

    def landed(n):
        for r in here[1 + 2 * n : 3 + 2 * n]:
            r.wait()
        for r in core[n]:
            r.wait_recv()

    here[0].wait()
    landed(0)
    unpack(0)
    for k in range(8, 0, -1):
        order = [(0, 1), (1, 0), (0, 0), (1, 1)] if k == 7 else [(0, 0), (1, 1)] if k == 8 else [(0, 0), (1, 0), (0, 1), (1, 1)]
        for d, h in order:
            slot = (slot_r if d == 0 else slot_l)(k)
            if (d, k, h) in gots:
                gots[d, k, h].wait_recv()
                add(slot, h, [(d, k)], A.at[slot, h])
            zsend(d, k, h)
        for d in (0, 1) if k < 8 else (0,):
            slot = (slot_r if d == 0 else slot_l)(k)
            if (d, k, 2) in gots:
                gots[d, k, 2].wait_recv()
                GA[slot] = add_gate(slot, [(d, k)])
            msend(d, k)
        if k == 8:
            landed(1)
        if k == 7:
            landed(2)
        if k > 1:
            unpack(k - 1)
        if k == 4:
            for r in wl:
                r.wait()
            for r in w1:
                r.wait_recv()

            @pl.loop(0, D, step=32)
            def _(at):
                rows = pl.ds(pl.multiple_of(at, 32), 32)
                total = OU[rows].astype(F32)
                for i in range(3):
                    total += RU[i, rows].astype(F32)
                SU[rows] = total.astype(BF)

            @pl.loop(0, NY)
            def _(j):
                @pl.loop(0, FF, step=64)
                def _(at):
                    rows = pl.ds(pl.multiple_of(at, 64), 64)
                    total = OD[j, rows].astype(F32)
                    for i in range(3):
                        total += RD[i, j, rows].astype(F32)
                    SD[j, rows] = total.astype(BF)

            w2 = [remote(SU.at[xcols[i + 1]], RU2.at[i], ws.at[6 + i], wr.at[6 + i], xs[i]) for i in range(3)]
            w2 += [remote(SD.at[yat[i + 1]], RD2.at[i], ws.at[9 + i], wr.at[9 + i], ys[i]) for i in range(3)]
            for r in w2:
                r.start()
        if k == 2:
            for r in w2:
                r.wait_recv()

            @pl.loop(0, 256, step=32)
            def _(at):
                rows = pl.ds(pl.multiple_of(at, 32), 32)
                total = SU[pl.ds(pl.multiple_of(x * 256 + at, 32), 32)].astype(F32)
                for i in range(3):
                    total += RU2[i, rows].astype(F32)
                SU2[rows] = total.astype(BF)

            @pl.loop(0, FF, step=64)
            def _(at):
                rows = pl.ds(pl.multiple_of(at, 64), 64)
                total = SD[y, rows].astype(F32)
                for i in range(3):
                    total += RD2[i, rows].astype(F32)
                SD2[rows] = total.astype(BF)

            theirs = pl.ds(pl.multiple_of((1 - c) * 128, 128), 128)
            w3 = [
                remote(SU2.at[theirs], RU3, ws.at[12], wr.at[12], sib),
                remote(SD2.at[:, theirs], RD3, ws.at[13], wr.at[13], sib),
            ]
            for r in w3:
                r.start()
    for r in w3:
        r.wait_recv()
    mine = pl.ds(pl.multiple_of(c * 128, 128), 128)
    last = [
        pltpu.make_async_copy(SU2.at[mine], UG.at[c], loc.at[9]),
        pltpu.make_async_copy(RU3, UG.at[1 - c], loc.at[10]),
        pltpu.make_async_copy(SD2.at[:, mine], DG.at[c], loc.at[11]),
        pltpu.make_async_copy(RD3, DG.at[1 - c], loc.at[12]),
    ]
    for r in last:
        r.start()
    for h in (0, 1):
        for d in (0, 1):
            gots[d, 0, h].wait_recv()
        add(0, h, [(0, 0), (1, 0)], FV.at[h])
        r = pltpu.make_async_copy(FV.at[h], F.at[h], loc.at[13 + h])
        r.start()
        last.append(r)
    for d in (0, 1):
        gots[d, 0, 2].wait_recv()
    GF[...] = add_gate(0, [(0, 0), (1, 0)])
    r = pltpu.make_async_copy(GF, GO, loc.at[15])
    r.start()
    last.append(r)
    for r in sends + w1 + w2 + w3 + [r for pair in core for r in pair]:
        r.wait_send()
    for r in last:
        r.wait()


def out_kernel(F, G, UG, DG, mixed, back, gate, upg, dng):
    mixed[...] = F[0]
    back[...] = F[1]
    gate[...] = G[0:TOP]
    upg[...] = UG[...].astype(F32)
    dng[...] = DG[...].astype(F32)


def shards(tokens, expert_ids, gates, w_up, w_down, out_grad):
    dma = pltpu.SemaphoreType.DMA
    sd = jax.ShapeDtypeStruct
    vm = pltpu.VMEM
    X, M, WU, WD = pl.pallas_call(
        ag_kernel,
        name="gather",
        out_shape=(
            sd((3, NY, 256, D), BF),
            sd((NZ, 16, TOK), BF),
            sd((NY, D, FF), BF),
            sd((NY, FF, D), BF),
        ),
        in_specs=[ANY, ANY, VM, VM, ANY, ANY],
        out_specs=[ANY] * 4,
        scratch_shapes=[vm((NZ, 2, TOK, D), BF), vm((NZ, 16, TOK), BF), vm((8, 2, 3, NY, 16, D), BF)]
        + [dma((2, 8, 2))] * 2 + [dma((2, 8))] * 2 + [dma((8,))] * 3 + [dma((14,))] * 2 + [dma((5,))],
        compiler_params=pltpu.CompilerParams(collective_id=1, has_side_effects=True, vmem_limit_bytes=60 << 20),
    )(tokens, out_grad, expert_ids.T, gates.T, w_up, w_down)

    O, S, PU, PD = pl.pallas_call(
        mid_kernel,
        name="experts",
        grid=(NY,),
        out_shape=(
            sd((2, NY, 256, D), BF),
            sd((NY, 256, 128), F32),
            sd((NY, D, FF), BF),
            sd((NY, FF, D), BF),
        ),
        in_specs=[
            pl.BlockSpec((3, 1, 256, D), lambda i: (0, i, 0, 0)),
            pl.BlockSpec((1, D, FF), lambda i: (i, 0, 0)),
            pl.BlockSpec((1, FF, D), lambda i: (i, 0, 0)),
        ],
        out_specs=[
            pl.BlockSpec((2, 1, 256, D), lambda i: (0, i, 0, 0)),
            pl.BlockSpec((1, 256, 128), lambda i: (i, 0, 0)),
            pl.BlockSpec((1, D, FF), lambda i: (i, 0, 0)),
            pl.BlockSpec((1, FF, D), lambda i: (i, 0, 0)),
        ],
        compiler_params=pltpu.CompilerParams(vmem_limit_bytes=60 << 20, dimension_semantics=("arbitrary",)),
    )(X, WU, WD)

    parts = pl.pallas_call(
        rs_kernel,
        name="scatter",
        out_shape=(
            sd((2, TOK, D), BF),
            sd((16, TOK), BF),
            sd((2, D // 8, FF), BF),
            sd((2, FF, D // 8), BF),
        ),
        in_specs=[ANY] * 5,
        out_specs=[ANY] * 4,
        scratch_shapes=[
            vm((2, 2, NY, 128, D), BF), vm((2, NY, 128, 128), F32), vm((NZ, 16, TOK), BF),
            vm((NZ, 2, TOK, D), BF), vm((2, 8, 2, TOK, D), BF),
            vm((NZ, 16, TOK), BF), vm((2, 8, 16, TOK), BF), vm((2, TOK, D), BF), vm((16, TOK), BF),
            vm((3, D, FF), BF), vm((D, FF), BF), vm((D, FF), BF), vm((3, 256, FF), BF), vm((256, FF), BF), vm((128, FF), BF),
            vm((3, NY, FF, 256), BF), vm((NY, FF, 256), BF), vm((NY, FF, 256), BF), vm((3, FF, 256), BF), vm((FF, 256), BF), vm((FF, 128), BF),
        ] + [dma((2, 8, 2))] * 2 + [dma((2, 8))] * 2 + [dma((6,))] * 2 + [dma((14,))] * 2 + [dma((16,))],
        compiler_params=pltpu.CompilerParams(collective_id=2, has_side_effects=True, vmem_limit_bytes=60 << 20),
    )(O, S, M, PU, PD)

    mixed, back, gate, upg, dng = pl.pallas_call(
        out_kernel,
        name="outputs",
        out_shape=(
            sd((TOK, D), BF),
            sd((TOK, D), BF),
            sd((TOP, TOK), BF),
            sd((2, D // 8, FF), F32),
            sd((2, FF, D // 8), F32),
        ),
        in_specs=[VM] * 4,
        out_specs=[VM] * 5,
    )(*parts)
    return mixed, back, gate.T, upg, dng


def solution(mesh):
    rows = P(("dp", "expert"), None)
    up, down = P("expert", "dp", None), P("expert", None, "dp")
    return jax.shard_map(
        shards,
        mesh=mesh,
        in_specs=(rows, rows, rows, up, down, rows),
        out_specs=(rows, rows, rows, up, down),
        check_vma=False,
    )
```

time: 254 us -> 218 us (0.86)
  Pallas kernels: 238 us -> 217 us
  local copies, waits for them, and re-layouts: 9.94 us -> 0 us
  other arithmetic: 3.78 us -> 0 us
    pallas_call x3 -> x4, Pallas kernels: 238 us -> 217 us  [the longest x1 104 us: shards(): pl.pallas_call(ag_kernel, name='gather', out_shape=(sd((3, NY, 256, D), B...]
    unnamed x8 -> x0, local copies, waits for them, and re-layouts: 8.62 us -> none
where the time goes in v2:
time: 218 us
  Pallas kernels  217 us (100%)
    pallas_call x1, Pallas kernels, shards(): pl.pallas_call(ag_kernel, name='gather', out_shape=(sd((3, NY, 256, D), B...  104 us
    pallas_call x1, Pallas kernels, shards(): pl.pallas_call(rs_kernel, name='scatter', out_shape=(sd((2, TOK, D), BF),...  96.5 us
    pallas_call x1, Pallas kernels, shards(): pl.pallas_call(mid_kernel, name='experts', grid=(NY,), out_shape=(sd((2,...  13.6 us

profile of v2, /device:TPU:1, one launch (start us, length us, event | category | flops | bytes accessed | tf_op | source)
XLA Modules:
  0.0 217.5 jit_solution(15825646923776153251)
XLA Ops:
  0.6 104.4 %gather.1 = (bf16[3,4,256,1024]{3,2,1,0:T(8,128)(2,1)}, bf16[16,16,128]{2,1,0:T(8,128)(2,1)}, bf16[4,1024,512]{2,1,0:T(8,128)(2,1)}, bf16[4,512,1024]{2,1,0:T(8,128)(2,1)}) custom-call(bf16[128,1024]{1,0:T(8,128)(2,1)} %tok.1, bf16[128,1024]{1,0:T(8,128)(2,1)} %cot.1, s32[4,128]{1,0:T(4,128)} %bitcast.3, bf16[4,128]{1,0:T(4,128)(2,1)} %bitcast.4, ...), custom_call_target="tpu_custom_call" | custom-call | tf_op jit(solution)/shard_map/gather/pallas_call | solution.py:411
  105.0 13.6 %experts.1 = (bf16[2,4,256,1024]{3,2,1,0:T(8,128)(2,1)}, f32[4,256,128]{2,1,0:T(8,128)}, bf16[4,1024,512]{2,1,0:T(8,128)(2,1)}, bf16[4,512,1024]{2,1,0:T(8,128)(2,1)}) custom-call(bf16[3,4,256,1024]{3,2,1,0:T(8,128)(2,1)} %get-tuple-element.22.X, bf16[4,1024,512]{2,1,0:T(8,128)(2,1)} %get-tuple-element.23.WU, bf16[4,512,1024]{2,1,0:T(8,128)(2,1)} %get-tuple-element.24.WD), custom_call_target="tpu_custom_call" | custom-call | tf_op jit(solution)/shard_map/experts/pallas_call | solution.py:427
  118.6 96.5 %scatter.1 = (bf16[2,128,1024]{2,1,0:T(8,128)(2,1)}, bf16[16,128]{1,0:T(8,128)(2,1)}, bf16[2,128,512]{2,1,0:T(8,128)(2,1)}, bf16[2,512,128]{2,1,0:T(8,128)(2,1)}) custom-call(bf16[2,4,256,1024]{3,2,1,0:T(8,128)(2,1)} %get-tuple-element.25.O, f32[4,256,128]{2,1,0:T(8,128)} %get-tuple-element.26.S, bf16[16,16,128]{2,1,0:T(8,128)(2,1)} %get-tuple-element.27.MI, ...), custom_call_target="tpu_custom_call" | custom-call | tf_op jit(solution)/shard_map/scatter/pallas_call | solution.py:451
  215.2 2.4 %outputs.1 = (bf16[128,1024]{1,0:T(8,128)(2,1)}, bf16[128,1024]{1,0:T(8,128)(2,1)}, bf16[4,128]{1,0:T(4,128)(2,1)}, f32[2,128,512]{2,1,0:T(8,128)}, f32[2,512,128]{2,1,0:T(8,128)}) custom-call(bf16[2,128,1024]{2,1,0:T(8,128)(2,1)} %get-tuple-element.30.F, bf16[16,128]{1,0:T(8,128)(2,1)} %get-tuple-element.31.G, bf16[2,128,512]{2,1,0:T(8,128)(2,1)} %get-tuple-element.32.UG, ...), custom_call_target="tpu_custom_call" | custom-call | tf_op jit(solution)/shard_map/outputs/pallas_call | solution.py:472

commit v3 on v2

--- a/solution.py
+++ b/solution.py
@@ -67,9 +67,46 @@
     return (0, 15) if p == 0 else (2 * p - 1, 2 * p)
 
 
+PACKED = {(11, 1): 0, (12, 0): 0, (13, 0): 0, (13, 1): 8, (14, 0): 8, (14, 1): 0, (15, 0): 8, (15, 1): 8}
+ROWS = {None: TOK, 0: 80, 8: 48}
+
+
+def rows_of(slot, h):
+    return pl.ds(0, ROWS[PACKED.get((slot, h))])
+
+
+def ahead(m, z, d):
+    m = m.astype(F32)
+    ids, rank = m[0:4].astype(jnp.int32), m[4:8].astype(jnp.int32)
+    one, two = (lax.rem(z + (n if d == 0 else NZ - n), NZ) for n in (1, 2))
+    plane = ids >> 3
+    row = jnp.where(plane == one, 0, jnp.where(plane == two, 40, -1000)) + (ids & 7) * 5 + rank
+    r = lax.broadcasted_iota(jnp.int32, (80, TOK), 0)
+    return sum(jnp.where(r == row[k : k + 1], 1.0, 0.0) for k in range(TOP)).astype(BF)
+
+
+def settle(h, first, c):
+    r = lax.broadcasted_iota(jnp.int32, (128, TOK), 0)
+    rank = r & 7
+    at = (((r >> 4) & 3) * 2 + ((r >> 6) ^ c)) * 5 + rank + first
+    at = jnp.where((((r >> 3) & 1) == h) & (rank < 5), at, -1)
+    return jnp.where(lax.broadcasted_iota(jnp.int32, (128, TOK), 1) == at, 1.0, 0.0)
+
+
+def routes(slots, n, dense, c, gate=None):
+    made = []
+    for h, slot in enumerate(slots):
+        kind = PACKED.get((slot, n))
+        if kind is None:
+            made.append(dense[:, h * TOK : (h + 1) * TOK])
+        else:
+            made.append(settle(h, kind, c) if gate is None else settle(h, kind, c) * gate)
+    return jnp.concatenate(made, axis=1).astype(BF)
+
+
 def ag_kernel(
     tok, cot, ids, gates, wu, wd, X, MO, WU, WD,
-    T, M, B, zs, zr, ms, mr, ps, pr, lp, ws, wr, loc,
+    T, M, B, Q, zs, zr, ms, mr, ps, pr, lp, ws, wr, loc,
 ):
     x, y, z, c, right, left, sib, xs, ys = places()
     greet([right, left, sib] + xs + ys)
@@ -78,8 +115,16 @@
 
     def zsend(d, k, h):
         slot = slot_r if d == 0 else slot_l
-        src = own[h] if k == 1 else T.at[slot(k - 1), h]
-        r = remote(src, T.at[slot(k), h], zs.at[d, k - 1, h], zr.at[d, k - 1, h], right if d == 0 else left)
+        kind, rows = PACKED.get((slot(k), h)), rows_of(slot(k), h)
+        if kind == 0:
+            past, n = slot(k - 1), 2 * d + k - 6
+            Q[n] = jnp.dot(ahead(M[past], z, d), T[past, h], preferred_element_type=F32).astype(BF)
+            src = Q.at[n]
+        elif kind == 8:
+            src = T.at[slot(k - 1), h, pl.ds(32, 48)]
+        else:
+            src = own[h] if k == 1 else T.at[slot(k - 1), h]
+        r = remote(src, T.at[slot(k), h, rows], zs.at[d, k - 1, h], zr.at[d, k - 1, h], right if d == 0 else left)
         r.start()
         steps[d, k, h] = r
 
@@ -120,6 +165,8 @@
     ).astype(BF)
     for d in (0, 1):
         msend(d, 1)
+    for (slot, h), kind in PACKED.items():
+        T[slot, h, ROWS[kind] :] = jnp.zeros((TOK - ROWS[kind], D), BF)
     for r in wl:
         r.wait()
     for r in wc:
@@ -136,10 +183,9 @@
     def pack(p):
         a, b = pair_slots(p)
         hot, weight, _ = selection(M[a], M[b], z * 8, c)
-        hot = hot.astype(BF)
         gate = jnp.sum(weight, axis=1, keepdims=True)
-        t = jnp.dot(hot, jnp.concatenate([T[a, 0], T[b, 0]], axis=0), preferred_element_type=F32)
-        g = jnp.dot(hot, jnp.concatenate([T[a, 1], T[b, 1]], axis=0), preferred_element_type=F32)
+        t = jnp.dot(routes((a, b), 0, hot, c), jnp.concatenate([T[a, 0], T[b, 0]], axis=0), preferred_element_type=F32)
+        g = jnp.dot(routes((a, b), 1, hot, c), jnp.concatenate([T[a, 1], T[b, 1]], axis=0), preferred_element_type=F32)
         for n, v in enumerate((t.astype(BF), g.astype(BF), (g * gate).astype(BF))):
             for q in range(8):
                 B[p, q // 4, n, q % 4] = v[q * 16 : q * 16 + 16]
@@ -150,6 +196,12 @@
         packed.append((here, there))
 
     for k in range(1, 9):
+        for d in (0, 1):
+            if (d, k, 2) not in steps:
+                continue
+            steps[d, k, 2].wait_recv()
+            if k < 7 or (k == 7 and d == 0):
+                msend(d, k + 1)
         for h in (0, 1):
             for d in (0, 1):
                 if (d, k, h) not in steps:
@@ -157,12 +209,6 @@
                 steps[d, k, h].wait_recv()
                 if k < 7 or (k == 7 and h == d):
                     zsend(d, k + 1, h)
-        for d in (0, 1):
-            if (d, k, 2) not in steps:
-                continue
-            steps[d, k, 2].wait_recv()
-            if k < 7 or (k == 7 and d == 0):
-                msend(d, k + 1)
         if k == 1:
             for r in own_local:
                 r.wait()
@@ -240,7 +286,8 @@
 
     def zsend(d, k, h):
         slot = (slot_r if d == 0 else slot_l)(k)
-        r = remote(A.at[slot, h], V.at[d, k - 1, h], zs.at[d, k - 1, h], zr.at[d, k - 1, h], left if d == 0 else right)
+        rows = rows_of(slot, h)
+        r = remote(A.at[slot, h, rows], V.at[d, k - 1, h, rows], zs.at[d, k - 1, h], zr.at[d, k - 1, h], left if d == 0 else right)
         r.start()
         sends.append(r)
         gots[d, k - 1, h] = r
@@ -272,9 +319,10 @@
         hot, weight, eqs = selection(M[slots[0]], M[slots[1]], z * 8, c)
         rows = pl.ds(p * 16, 16)
         over = (((0,), (0,)), ((), ()))
-        for n, w in enumerate((weight, hot)):
+        gate = jnp.sum(weight, axis=1, keepdims=True)
+        for n, w in enumerate((routes(slots, 0, weight, c, gate), routes(slots, 1, hot, c))):
             v = jnp.concatenate([OL[q // 4, n, q % 4, rows] for q in range(8)], axis=0)
-            u = lax.dot_general(w.astype(BF), v, over, preferred_element_type=F32).astype(BF)
+            u = lax.dot_general(w, v, over, preferred_element_type=F32).astype(BF)
             for h, slot in enumerate(slots):
                 A[slot, n] = u[h * TOK : (h + 1) * TOK]
         dots = jnp.concatenate([SL[q // 4, q % 4, rows] for q in range(8)], axis=0)
@@ -297,7 +345,16 @@
             slot = (slot_r if d == 0 else slot_l)(k)
             if (d, k, h) in gots:
                 gots[d, k, h].wait_recv()
-                add(slot, h, [(d, k)], A.at[slot, h])
+                came = PACKED.get(((slot_r if d == 0 else slot_l)(k + 1), h))
+                if came is None:
+                    add(slot, h, [(d, k)], A.at[slot, h])
+                elif came == 8:
+                    total = A[slot, h, 32:80].astype(F32) + V[d, k, h, 0:48].astype(F32)
+                    A[slot, h, 32:80] = total.astype(BF)
+                else:
+                    hot = ahead(M[slot], z, d)
+                    total = lax.dot_general(hot, V[d, k, h, 0:80], (((0,), (0,)), ((), ())), preferred_element_type=F32)
+                    A[slot, h] = (total + A[slot, h].astype(F32)).astype(BF)
             zsend(d, k, h)
         for d in (0, 1) if k < 8 else (0,):
             slot = (slot_r if d == 0 else slot_l)(k)
@@ -419,7 +476,7 @@
         ),
         in_specs=[ANY, ANY, VM, VM, ANY, ANY],
         out_specs=[ANY] * 4,
-        scratch_shapes=[vm((NZ, 2, TOK, D), BF), vm((NZ, 16, TOK), BF), vm((8, 2, 3, NY, 16, D), BF)]
+        scratch_shapes=[vm((NZ, 2, TOK, D), BF), vm((NZ, 16, TOK), BF), vm((8, 2, 3, NY, 16, D), BF), vm((4, 80, D), BF)]
         + [dma((2, 8, 2))] * 2 + [dma((2, 8))] * 2 + [dma((8,))] * 3 + [dma((14,))] * 2 + [dma((5,))],
         compiler_params=pltpu.CompilerParams(collective_id=1, has_side_effects=True, vmem_limit_bytes=60 << 20),
     )(tokens, out_grad, expert_ids.T, gates.T, w_up, w_down)

time: 218 us -> 205 us (0.940)
  Pallas kernels: 217 us -> 204 us
    pallas_call x1, Pallas kernels: 104 us -> 96.5 us  [shards(): pl.pallas_call(ag_kernel, name='gather', out_shape=(sd((3, NY, 256, D), B...]
    pallas_call x1, Pallas kernels: 96.5 us -> 91.2 us  [shards(): pl.pallas_call(rs_kernel, name='scatter', out_shape=(sd((2, TOK, D), BF),...]
where the time goes in v3:
time: 205 us
  Pallas kernels  204 us (100%)
    pallas_call x1, Pallas kernels, shards(): pl.pallas_call(ag_kernel, name='gather', out_shape=(sd((3, NY, 256, D), B...  96.5 us
    pallas_call x1, Pallas kernels, shards(): pl.pallas_call(rs_kernel, name='scatter', out_shape=(sd((2, TOK, D), BF),...  91.2 us
    pallas_call x1, Pallas kernels, shards(): pl.pallas_call(mid_kernel, name='experts', grid=(NY,), out_shape=(sd((2,...  13.8 us

profile of v3, /device:TPU:1, one launch (start us, length us, event | category | flops | bytes accessed | tf_op | source)
XLA Modules:
  0.0 204.6 jit_solution(15916021699885619714)
XLA Ops:
  0.6 96.5 %gather.1 = (bf16[3,4,256,1024]{3,2,1,0:T(8,128)(2,1)}, bf16[16,16,128]{2,1,0:T(8,128)(2,1)}, bf16[4,1024,512]{2,1,0:T(8,128)(2,1)}, bf16[4,512,1024]{2,1,0:T(8,128)(2,1)}) custom-call(bf16[128,1024]{1,0:T(8,128)(2,1)} %tok.1, bf16[128,1024]{1,0:T(8,128)(2,1)} %cot.1, s32[4,128]{1,0:T(4,128)} %bitcast.3, bf16[4,128]{1,0:T(4,128)(2,1)} %bitcast.4, ...), custom_call_target="tpu_custom_call" | custom-call | tf_op jit(solution)/shard_map/gather/pallas_call | solution.py:468
  97.2 13.8 %experts.1 = (bf16[2,4,256,1024]{3,2,1,0:T(8,128)(2,1)}, f32[4,256,128]{2,1,0:T(8,128)}, bf16[4,1024,512]{2,1,0:T(8,128)(2,1)}, bf16[4,512,1024]{2,1,0:T(8,128)(2,1)}) custom-call(bf16[3,4,256,1024]{3,2,1,0:T(8,128)(2,1)} %get-tuple-element.22.X, bf16[4,1024,512]{2,1,0:T(8,128)(2,1)} %get-tuple-element.23.WU, bf16[4,512,1024]{2,1,0:T(8,128)(2,1)} %get-tuple-element.24.WD), custom_call_target="tpu_custom_call" | custom-call | tf_op jit(solution)/shard_map/experts/pallas_call | solution.py:484
  111.0 91.2 %scatter.1 = (bf16[2,128,1024]{2,1,0:T(8,128)(2,1)}, bf16[16,128]{1,0:T(8,128)(2,1)}, bf16[2,128,512]{2,1,0:T(8,128)(2,1)}, bf16[2,512,128]{2,1,0:T(8,128)(2,1)}) custom-call(bf16[2,4,256,1024]{3,2,1,0:T(8,128)(2,1)} %get-tuple-element.25.O, f32[4,256,128]{2,1,0:T(8,128)} %get-tuple-element.26.S, bf16[16,16,128]{2,1,0:T(8,128)(2,1)} %get-tuple-element.27.MI, ...), custom_call_target="tpu_custom_call" | custom-call | tf_op jit(solution)/shard_map/scatter/pallas_call | solution.py:508
  202.2 2.4 %outputs.1 = (bf16[128,1024]{1,0:T(8,128)(2,1)}, bf16[128,1024]{1,0:T(8,128)(2,1)}, bf16[4,128]{1,0:T(4,128)(2,1)}, f32[2,128,512]{2,1,0:T(8,128)}, f32[2,512,128]{2,1,0:T(8,128)}) custom-call(bf16[2,128,1024]{2,1,0:T(8,128)(2,1)} %get-tuple-element.30.F, bf16[16,128]{1,0:T(8,128)(2,1)} %get-tuple-element.31.G, bf16[2,128,512]{2,1,0:T(8,128)(2,1)} %get-tuple-element.32.UG, ...), custom_call_target="tpu_custom_call" | custom-call | tf_op jit(solution)/shard_map/outputs/pallas_call | solution.py:529

commit v4 on v3

--- a/solution.py
+++ b/solution.py
@@ -212,12 +212,12 @@
         if k == 1:
             for r in own_local:
                 r.wait()
-        if k == 2:
+        pack(k % 8)
+        if k == 1:
             for r in w1:
                 r.wait_recv()
             for r in w2:
                 r.start()
-        pack(k % 8)
     out = pltpu.make_async_copy(M, MO, loc.at[4])
     out.start()
     for r in w2:
@@ -368,7 +368,7 @@
             landed(2)
         if k > 1:
             unpack(k - 1)
-        if k == 4:
+        if k == 2:
             for r in wl:
                 r.wait()
             for r in w1:
@@ -396,7 +396,7 @@
             w2 += [remote(SD.at[yat[i + 1]], RD2.at[i], ws.at[9 + i], wr.at[9 + i], ys[i]) for i in range(3)]
             for r in w2:
                 r.start()
-        if k == 2:
+        if k == 1:
             for r in w2:
                 r.wait_recv()
 

time: 205 us -> 199 us (0.971)
  Pallas kernels: 204 us -> 198 us
    pallas_call x1, Pallas kernels: 91.2 us -> 85.7 us  [shards(): pl.pallas_call(rs_kernel, name='scatter', out_shape=(sd((2, TOK, D), BF),...]
where the time goes in v4:
time: 199 us
  Pallas kernels  198 us (99%)
    pallas_call x1, Pallas kernels, shards(): pl.pallas_call(ag_kernel, name='gather', out_shape=(sd((3, NY, 256, D), B...  96.5 us
    pallas_call x1, Pallas kernels, shards(): pl.pallas_call(rs_kernel, name='scatter', out_shape=(sd((2, TOK, D), BF),...  85.7 us
    pallas_call x1, Pallas kernels, shards(): pl.pallas_call(mid_kernel, name='experts', grid=(NY,), out_shape=(sd((2,...  13.8 us

profile of v4, /device:TPU:1, one launch (start us, length us, event | category | flops | bytes accessed | tf_op | source)
XLA Modules:
  0.0 199.0 jit_solution(8454084159554897257)
XLA Ops:
  0.6 96.5 %gather.1 = (bf16[3,4,256,1024]{3,2,1,0:T(8,128)(2,1)}, bf16[16,16,128]{2,1,0:T(8,128)(2,1)}, bf16[4,1024,512]{2,1,0:T(8,128)(2,1)}, bf16[4,512,1024]{2,1,0:T(8,128)(2,1)}) custom-call(bf16[128,1024]{1,0:T(8,128)(2,1)} %tok.1, bf16[128,1024]{1,0:T(8,128)(2,1)} %cot.1, s32[4,128]{1,0:T(4,128)} %bitcast.3, bf16[4,128]{1,0:T(4,128)(2,1)} %bitcast.4, ...), custom_call_target="tpu_custom_call" | custom-call | tf_op jit(solution)/shard_map/gather/pallas_call | solution.py:468
  97.2 13.8 %experts.1 = (bf16[2,4,256,1024]{3,2,1,0:T(8,128)(2,1)}, f32[4,256,128]{2,1,0:T(8,128)}, bf16[4,1024,512]{2,1,0:T(8,128)(2,1)}, bf16[4,512,1024]{2,1,0:T(8,128)(2,1)}) custom-call(bf16[3,4,256,1024]{3,2,1,0:T(8,128)(2,1)} %get-tuple-element.22.X, bf16[4,1024,512]{2,1,0:T(8,128)(2,1)} %get-tuple-element.23.WU, bf16[4,512,1024]{2,1,0:T(8,128)(2,1)} %get-tuple-element.24.WD), custom_call_target="tpu_custom_call" | custom-call | tf_op jit(solution)/shard_map/experts/pallas_call | solution.py:484
  111.0 85.7 %scatter.1 = (bf16[2,128,1024]{2,1,0:T(8,128)(2,1)}, bf16[16,128]{1,0:T(8,128)(2,1)}, bf16[2,128,512]{2,1,0:T(8,128)(2,1)}, bf16[2,512,128]{2,1,0:T(8,128)(2,1)}) custom-call(bf16[2,4,256,1024]{3,2,1,0:T(8,128)(2,1)} %get-tuple-element.25.O, f32[4,256,128]{2,1,0:T(8,128)} %get-tuple-element.26.S, bf16[16,16,128]{2,1,0:T(8,128)(2,1)} %get-tuple-element.27.MI, ...), custom_call_target="tpu_custom_call" | custom-call | tf_op jit(solution)/shard_map/scatter/pallas_call | solution.py:508
  196.7 2.4 %outputs.1 = (bf16[128,1024]{1,0:T(8,128)(2,1)}, bf16[128,1024]{1,0:T(8,128)(2,1)}, bf16[4,128]{1,0:T(4,128)(2,1)}, f32[2,128,512]{2,1,0:T(8,128)}, f32[2,512,128]{2,1,0:T(8,128)}) custom-call(bf16[2,128,1024]{2,1,0:T(8,128)(2,1)} %get-tuple-element.30.F, bf16[16,128]{1,0:T(8,128)(2,1)} %get-tuple-element.31.G, bf16[2,128,512]{2,1,0:T(8,128)(2,1)} %get-tuple-element.32.UG, ...), custom_call_target="tpu_custom_call" | custom-call | tf_op jit(solution)/shard_map/outputs/pallas_call | solution.py:529

commit v5 on v4

--- a/solution.py
+++ b/solution.py
@@ -180,12 +180,16 @@
 
     packed = []
 
-    def pack(p):
+    def choose(p):
         a, b = pair_slots(p)
         hot, weight, _ = selection(M[a], M[b], z * 8, c)
-        gate = jnp.sum(weight, axis=1, keepdims=True)
-        t = jnp.dot(routes((a, b), 0, hot, c), jnp.concatenate([T[a, 0], T[b, 0]], axis=0), preferred_element_type=F32)
-        g = jnp.dot(routes((a, b), 1, hot, c), jnp.concatenate([T[a, 1], T[b, 1]], axis=0), preferred_element_type=F32)
+        return routes((a, b), 0, hot, c), routes((a, b), 1, hot, c), jnp.sum(weight, axis=1, keepdims=True)
+
+    def pack(p, chosen):
+        a, b = pair_slots(p)
+        for_tok, for_cot, gate = chosen
+        t = jnp.dot(for_tok, jnp.concatenate([T[a, 0], T[b, 0]], axis=0), preferred_element_type=F32)
+        g = jnp.dot(for_cot, jnp.concatenate([T[a, 1], T[b, 1]], axis=0), preferred_element_type=F32)
         for n, v in enumerate((t.astype(BF), g.astype(BF), (g * gate).astype(BF))):
             for q in range(8):
                 B[p, q // 4, n, q % 4] = v[q * 16 : q * 16 + 16]
@@ -202,6 +206,7 @@
             steps[d, k, 2].wait_recv()
             if k < 7 or (k == 7 and d == 0):
                 msend(d, k + 1)
+        chosen = choose(0) if k == 8 else None
         for h in (0, 1):
             for d in (0, 1):
                 if (d, k, h) not in steps:
@@ -212,7 +217,7 @@
         if k == 1:
             for r in own_local:
                 r.wait()
-        pack(k % 8)
+        pack(k % 8, chosen or choose(k))
         if k == 1:
             for r in w1:
                 r.wait_recv()
@@ -230,56 +235,66 @@
     out.wait()
 
 
-def mid_kernel(X, WU, WD, O, S, PU, PD):
-    x, cot, scaled, wu, wd = X[0, 0], X[1, 0], X[2, 0], WU[0], WD[0]
-    pre = jnp.dot(x, wu, preferred_element_type=F32)
-    t = jnp.tanh(0.7978845608 * (pre + 0.044715 * pre * pre * pre))
-    act = (0.5 * pre * (1.0 + t)).astype(BF)
-    slope = 0.5 * (1.0 + t) + 0.5 * pre * (1.0 - t * t) * (0.7978845608 * (1.0 + 0.134145 * pre * pre))
-    act_grad = lax.dot_general(scaled, wd, (((1,), (1,)), ((), ())), preferred_element_type=F32)
-    pre_grad = (act_grad * slope).astype(BF)
-    outs = jnp.dot(act, wd, preferred_element_type=F32).astype(BF)
-    O[0, 0] = outs
-    S[0] = jnp.broadcast_to(jnp.sum(cot.astype(F32) * outs.astype(F32), axis=1, keepdims=True), (256, 128))
-    O[1, 0] = lax.dot_general(pre_grad, wu, (((1,), (1,)), ((), ())), preferred_element_type=F32).astype(BF)
-    PU[0] = lax.dot_general(x, pre_grad, (((0,), (0,)), ((), ())), preferred_element_type=F32).astype(BF)
-    PD[0] = lax.dot_general(act, scaled, (((0,), (0,)), ((), ())), preferred_element_type=F32).astype(BF)
-
-
 def rs_kernel(
-    O, S, MI, PU, PD, F, GO, UG, DG,
-    OL, SL, M, A, V, GA, GV, FV, GF, RU, OU, SU, RU2, SU2, RU3, RD, OD, SD, RD2, SD2, RD3,
-    zs, zr, ms, mr, cs, cr, ws, wr, loc,
+    X, MI, WU, WD, F, GO, UG, DG,
+    XV, WUV, WDV, OB, OR, SB, SR, AC, PG, PU, PD,
+    M, A, V, GA, GV, FV, GF, RU, SU, RU2, SU2, RU3, RD, OD, SD, RD2, SD2, RD3,
+    zs, zr, ms, mr, cs, cr, ws, wr, loc, ld,
 ):
     x, y, z, c, right, left, sib, xs, ys = places()
+    loads = {}
+
+    def load(e):
+        loads[e] = [
+            pltpu.make_async_copy(X.at[:, e], XV.at[:, e], ld.at[e, 0]),
+            pltpu.make_async_copy(WU.at[e], WUV.at[e % 2], ld.at[e, 1]),
+            pltpu.make_async_copy(WD.at[e], WDV.at[e % 2], ld.at[e, 2]),
+        ]
+        for r in loads[e]:
+            r.start()
+
+    load(0)
+    load(1)
+    near = pltpu.make_async_copy(MI, M, loc.at[0])
+    near.start()
     greet([right, left, sib] + xs + ys)
-    parts = [(0, 16), (112, 16), (16, 96)]
-    core, here = [], [pltpu.make_async_copy(MI, M, loc.at[0])]
-    here[0].start()
-    for n, (at, size) in enumerate(parts):
-        a, b = pl.ds(at, size), pl.ds(128 + at, size)
+    core = []
+    for e in range(NY):
+        for r in loads[e]:
+            r.wait()
+        rows, cot, scaled, wu, wd = XV[0, e], XV[1, e], XV[2, e], WUV[e % 2], WDV[e % 2]
+        pre = jnp.dot(rows, wu, preferred_element_type=F32)
+        t = jnp.tanh(0.7978845608 * (pre + 0.044715 * pre * pre * pre))
+        act = (0.5 * pre * (1.0 + t)).astype(BF)
+        slope = 0.5 * (1.0 + t) + 0.5 * pre * (1.0 - t * t) * (0.7978845608 * (1.0 + 0.134145 * pre * pre))
+        act_grad = lax.dot_general(scaled, wd, (((1,), (1,)), ((), ())), preferred_element_type=F32)
+        pre_grad = (act_grad * slope).astype(BF)
+        outs = jnp.dot(act, wd, preferred_element_type=F32).astype(BF)
+        OB[0, e] = outs
+        SB[e] = jnp.broadcast_to(jnp.sum(cot.astype(F32) * outs.astype(F32), axis=1, keepdims=True), (256, 128))
+        OB[1, e] = lax.dot_general(pre_grad, wu, (((1,), (1,)), ((), ())), preferred_element_type=F32).astype(BF)
+        AC[e] = act
+        PG[e] = pre_grad
         pair = [
-            remote(O.at[:, :, b], OL.at[1, :, :, a], cs.at[n], cr.at[n], sib),
-            remote(S.at[:, b], SL.at[1, :, a], cs.at[3 + n], cr.at[3 + n], sib),
+            remote(OB.at[:, e, pl.ds(128, 128)], OR.at[:, e], cs.at[e], cr.at[e], sib),
+            remote(SB.at[e, pl.ds(128, 128)], SR.at[e], cs.at[4 + e], cr.at[4 + e], sib),
         ]
-        mine = [
-            pltpu.make_async_copy(O.at[:, :, a], OL.at[0, :, :, a], loc.at[1 + n]),
-            pltpu.make_async_copy(S.at[:, a], SL.at[0, :, a], loc.at[4 + n]),
-        ]
-        for r in pair + mine:
+        for r in pair:
             r.start()
-        core.append(pair)
-        here += mine
+        core += pair
+        if e < 2:
+            load(e + 2)
+
+    def weigh(e):
+        over = (((0,), (0,)), ((), ()))
+        PU[e] = lax.dot_general(XV[0, e], PG[e], over, preferred_element_type=F32).astype(BF)
+        PD[e] = lax.dot_general(AC[e], XV[2, e], over, preferred_element_type=F32).astype(BF)
+
     xcols = [pl.ds(pl.multiple_of(lax.rem(x + i, NX) * 256, 256), 256) for i in range(NX)]
     yat = [lax.rem(y + i, NY) for i in range(NY)]
     w1 = [remote(PU.at[yat[i + 1]], RU.at[i], ws.at[i], wr.at[i], ys[i]) for i in range(3)]
     w1 += [remote(PD.at[:, :, xcols[i + 1]], RD.at[i], ws.at[3 + i], wr.at[3 + i], xs[i]) for i in range(3)]
-    wl = [
-        pltpu.make_async_copy(PU.at[y], OU, loc.at[7]),
-        pltpu.make_async_copy(PD.at[:, :, xcols[0]], OD, loc.at[8]),
-    ]
-    for r in w1 + wl:
-        r.start()
+    wl = [pltpu.make_async_copy(PD.at[:, :, xcols[0]], OD, loc.at[8])]
 
     sends = []
     gots = {}
@@ -314,31 +329,28 @@
             total += GV[d, k].astype(F32)
         return total.astype(BF)
 
-    def unpack(p):
+    def unpack(p, first=False):
         slots = pair_slots(p)
         hot, weight, eqs = selection(M[slots[0]], M[slots[1]], z * 8, c)
         rows = pl.ds(p * 16, 16)
         over = (((0,), (0,)), ((), ()))
         gate = jnp.sum(weight, axis=1, keepdims=True)
-        for n, w in enumerate((routes(slots, 0, weight, c, gate), routes(slots, 1, hot, c))):
-            v = jnp.concatenate([OL[q // 4, n, q % 4, rows] for q in range(8)], axis=0)
+        ways = (routes(slots, 0, weight, c, gate), routes(slots, 1, hot, c))
+        if first:
+            for r in core:
+                r.wait_recv()
+        for n, w in enumerate(ways):
+            v = jnp.concatenate([b[n, q, rows] for b in (OB, OR) for q in range(NY)], axis=0)
             u = lax.dot_general(w, v, over, preferred_element_type=F32).astype(BF)
             for h, slot in enumerate(slots):
                 A[slot, n] = u[h * TOK : (h + 1) * TOK]
-        dots = jnp.concatenate([SL[q // 4, q % 4, rows] for q in range(8)], axis=0)
+        dots = jnp.concatenate([b[q, rows] for b in (SB, SR) for q in range(NY)], axis=0)
         for h, slot in enumerate(slots):
             gp = [jnp.sum(jnp.where(eq, dots, 0.0), axis=0, keepdims=True) for eq in eqs[h]]
             GA[slot] = jnp.concatenate(gp + [jnp.zeros((12, TOK), F32)], axis=0).astype(BF)
 
-    def landed(n):
-        for r in here[1 + 2 * n : 3 + 2 * n]:
-            r.wait()
-        for r in core[n]:
-            r.wait_recv()
-
-    here[0].wait()
-    landed(0)
-    unpack(0)
+    near.wait()
+    unpack(0, True)
     for k in range(8, 0, -1):
         order = [(0, 1), (1, 0), (0, 0), (1, 1)] if k == 7 else [(0, 0), (1, 1)] if k == 8 else [(0, 0), (1, 0), (0, 1), (1, 1)]
         for d, h in order:
@@ -362,12 +374,14 @@
                 gots[d, k, 2].wait_recv()
                 GA[slot] = add_gate(slot, [(d, k)])
             msend(d, k)
-        if k == 8:
-            landed(1)
-        if k == 7:
-            landed(2)
         if k > 1:
             unpack(k - 1)
+        if k in (7, 6):
+            weigh(2 * (7 - k))
+            weigh(2 * (7 - k) + 1)
+        if k == 6:
+            for r in w1 + wl:
+                r.start()
         if k == 2:
             for r in wl:
                 r.wait()
@@ -377,7 +391,7 @@
             @pl.loop(0, D, step=32)
             def _(at):
                 rows = pl.ds(pl.multiple_of(at, 32), 32)
-                total = OU[rows].astype(F32)
+                total = PU[y, rows].astype(F32)
                 for i in range(3):
                     total += RU[i, rows].astype(F32)
                 SU[rows] = total.astype(BF)
@@ -447,7 +461,7 @@
     r = pltpu.make_async_copy(GF, GO, loc.at[15])
     r.start()
     last.append(r)
-    for r in sends + w1 + w2 + w3 + [r for pair in core for r in pair]:
+    for r in sends + w1 + w2 + w3 + core:
         r.wait_send()
     for r in last:
         r.wait()
@@ -481,30 +495,6 @@
         compiler_params=pltpu.CompilerParams(collective_id=1, has_side_effects=True, vmem_limit_bytes=60 << 20),
     )(tokens, out_grad, expert_ids.T, gates.T, w_up, w_down)
 
-    O, S, PU, PD = pl.pallas_call(
-        mid_kernel,
-        name="experts",
-        grid=(NY,),
-        out_shape=(
-            sd((2, NY, 256, D), BF),
-            sd((NY, 256, 128), F32),
-            sd((NY, D, FF), BF),
-            sd((NY, FF, D), BF),
-        ),
-        in_specs=[
-            pl.BlockSpec((3, 1, 256, D), lambda i: (0, i, 0, 0)),
-            pl.BlockSpec((1, D, FF), lambda i: (i, 0, 0)),
-            pl.BlockSpec((1, FF, D), lambda i: (i, 0, 0)),
-        ],
-        out_specs=[
-            pl.BlockSpec((2, 1, 256, D), lambda i: (0, i, 0, 0)),
-            pl.BlockSpec((1, 256, 128), lambda i: (i, 0, 0)),
-            pl.BlockSpec((1, D, FF), lambda i: (i, 0, 0)),
-            pl.BlockSpec((1, FF, D), lambda i: (i, 0, 0)),
-        ],
-        compiler_params=pltpu.CompilerParams(vmem_limit_bytes=60 << 20, dimension_semantics=("arbitrary",)),
-    )(X, WU, WD)
-
     parts = pl.pallas_call(
         rs_kernel,
         name="scatter",
@@ -514,17 +504,19 @@
             sd((2, D // 8, FF), BF),
             sd((2, FF, D // 8), BF),
         ),
-        in_specs=[ANY] * 5,
+        in_specs=[ANY] * 4,
         out_specs=[ANY] * 4,
         scratch_shapes=[
-            vm((2, 2, NY, 128, D), BF), vm((2, NY, 128, 128), F32), vm((NZ, 16, TOK), BF),
-            vm((NZ, 2, TOK, D), BF), vm((2, 8, 2, TOK, D), BF),
+            vm((3, NY, 256, D), BF), vm((2, D, FF), BF), vm((2, FF, D), BF),
+            vm((2, NY, 256, D), BF), vm((2, NY, 128, D), BF), vm((NY, 256, 128), F32), vm((NY, 128, 128), F32),
+            vm((NY, 256, FF), BF), vm((NY, 256, FF), BF), vm((NY, D, FF), BF), vm((NY, FF, D), BF),
+            vm((NZ, 16, TOK), BF), vm((NZ, 2, TOK, D), BF), vm((2, 8, 2, TOK, D), BF),
             vm((NZ, 16, TOK), BF), vm((2, 8, 16, TOK), BF), vm((2, TOK, D), BF), vm((16, TOK), BF),
-            vm((3, D, FF), BF), vm((D, FF), BF), vm((D, FF), BF), vm((3, 256, FF), BF), vm((256, FF), BF), vm((128, FF), BF),
+            vm((3, D, FF), BF), vm((D, FF), BF), vm((3, 256, FF), BF), vm((256, FF), BF), vm((128, FF), BF),
             vm((3, NY, FF, 256), BF), vm((NY, FF, 256), BF), vm((NY, FF, 256), BF), vm((3, FF, 256), BF), vm((FF, 256), BF), vm((FF, 128), BF),
-        ] + [dma((2, 8, 2))] * 2 + [dma((2, 8))] * 2 + [dma((6,))] * 2 + [dma((14,))] * 2 + [dma((16,))],
+        ] + [dma((2, 8, 2))] * 2 + [dma((2, 8))] * 2 + [dma((8,))] * 2 + [dma((14,))] * 2 + [dma((16,)), dma((NY, 3))],
         compiler_params=pltpu.CompilerParams(collective_id=2, has_side_effects=True, vmem_limit_bytes=60 << 20),
-    )(O, S, M, PU, PD)
+    )(X, M, WU, WD)
 
     mixed, back, gate, upg, dng = pl.pallas_call(
         out_kernel,

time: 199 us -> 192 us (0.965)
  Pallas kernels: 198 us -> 191 us
    pallas_call x1 -> x0, Pallas kernels: 13.8 us -> none  [shards(): pl.pallas_call(mid_kernel, name='experts', grid=(NY,), out_shape=(sd((2,...]
    pallas_call x1, Pallas kernels: 85.7 us -> 92.2 us  [shards(): pl.pallas_call(rs_kernel, name='scatter', out_shape=(sd((2, TOK, D), BF),...]
where the time goes in v5:
time: 192 us
  Pallas kernels  191 us (99%)
    pallas_call x1, Pallas kernels, shards(): pl.pallas_call(ag_kernel, name='gather', out_shape=(sd((3, NY, 256, D), B...  96.5 us
    pallas_call x1, Pallas kernels, shards(): pl.pallas_call(rs_kernel, name='scatter', out_shape=(sd((2, TOK, D), BF),...  92.2 us

profile of v5, /device:TPU:1, one launch (start us, length us, event | category | flops | bytes accessed | tf_op | source)
XLA Modules:
  0.0 191.7 jit_solution(15215599597672910181)
XLA Ops:
  0.6 96.5 %gather.1 = (bf16[3,4,256,1024]{3,2,1,0:T(8,128)(2,1)}, bf16[16,16,128]{2,1,0:T(8,128)(2,1)}, bf16[4,1024,512]{2,1,0:T(8,128)(2,1)}, bf16[4,512,1024]{2,1,0:T(8,128)(2,1)}) custom-call(bf16[128,1024]{1,0:T(8,128)(2,1)} %tok.1, bf16[128,1024]{1,0:T(8,128)(2,1)} %cot.1, s32[4,128]{1,0:T(4,128)} %bitcast.3, bf16[4,128]{1,0:T(4,128)(2,1)} %bitcast.4, ...), custom_call_target="tpu_custom_call" | custom-call | tf_op jit(solution)/shard_map/gather/pallas_call | solution.py:482
  97.2 92.2 %scatter.1 = (bf16[2,128,1024]{2,1,0:T(8,128)(2,1)}, bf16[16,128]{1,0:T(8,128)(2,1)}, bf16[2,128,512]{2,1,0:T(8,128)(2,1)}, bf16[2,512,128]{2,1,0:T(8,128)(2,1)}) custom-call(bf16[3,4,256,1024]{3,2,1,0:T(8,128)(2,1)} %get-tuple-element.18.X, bf16[16,16,128]{2,1,0:T(8,128)(2,1)} %get-tuple-element.19.MI, bf16[4,1024,512]{2,1,0:T(8,128)(2,1)} %get-tuple-element.20.WU, ...), custom_call_target="tpu_custom_call" | custom-call | tf_op jit(solution)/shard_map/scatter/pallas_call | solution.py:498
  189.4 2.4 %outputs.1 = (bf16[128,1024]{1,0:T(8,128)(2,1)}, bf16[128,1024]{1,0:T(8,128)(2,1)}, bf16[4,128]{1,0:T(4,128)(2,1)}, f32[2,128,512]{2,1,0:T(8,128)}, f32[2,512,128]{2,1,0:T(8,128)}) custom-call(bf16[2,128,1024]{2,1,0:T(8,128)(2,1)} %get-tuple-element.22.F, bf16[16,128]{1,0:T(8,128)(2,1)} %get-tuple-element.23.G, bf16[2,128,512]{2,1,0:T(8,128)(2,1)} %get-tuple-element.24.UG, ...), custom_call_target="tpu_custom_call" | custom-call | tf_op jit(solution)/shard_map/outputs/pallas_call | solution.py:521

commit v6 on v5

--- a/solution.py
+++ b/solution.py
@@ -75,6 +75,10 @@
     return pl.ds(0, ROWS[PACKED.get((slot, h))])
 
 
+def blocks_of(slot, h):
+    return [rows_of(slot, h)] if (slot, h) in PACKED else [pl.ds(0, 64), pl.ds(64, 64)]
+
+
 def ahead(m, z, d):
     m = m.astype(F32)
     ids, rank = m[0:4].astype(jnp.int32), m[4:8].astype(jnp.int32)
@@ -113,9 +117,9 @@
     own = (tok, cot)
     steps = {}
 
-    def zsend(d, k, h):
+    def zsend(d, k, h, part):
         slot = slot_r if d == 0 else slot_l
-        kind, rows = PACKED.get((slot(k), h)), rows_of(slot(k), h)
+        kind, rows = PACKED.get((slot(k), h)), blocks_of(slot(k), h)[part]
         if kind == 0:
             past, n = slot(k - 1), 2 * d + k - 6
             Q[n] = jnp.dot(ahead(M[past], z, d), T[past, h], preferred_element_type=F32).astype(BF)
@@ -123,10 +127,11 @@
         elif kind == 8:
             src = T.at[slot(k - 1), h, pl.ds(32, 48)]
         else:
-            src = own[h] if k == 1 else T.at[slot(k - 1), h]
-        r = remote(src, T.at[slot(k), h, rows], zs.at[d, k - 1, h], zr.at[d, k - 1, h], right if d == 0 else left)
-        r.start()
-        steps[d, k, h] = r
+            src = own[h].at[rows] if k == 1 else T.at[slot(k - 1), h, rows]
+        at = (d, k - 1, h, part)
+        r = remote(src, T.at[slot(k), h, rows], zs.at[at], zr.at[at], right if d == 0 else left)
+        r.start()
+        steps[d, k, h, part] = r
 
     def msend(d, k):
         slot = slot_r if d == 0 else slot_l
@@ -136,8 +141,9 @@
         steps[d, k, 2] = r
 
     for h in (0, 1):
-        for d in (0, 1):
-            zsend(d, 1, h)
+        for part in (0, 1):
+            for d in (0, 1):
+                zsend(d, 1, h, part)
     rows1 = pl.ds(pl.multiple_of(x * 256 + c * 128, 128), 128)
     rows2 = pl.ds(pl.multiple_of(x * 256, 256), 256)
     wl = [
@@ -208,12 +214,18 @@
                 msend(d, k + 1)
         chosen = choose(0) if k == 8 else None
         for h in (0, 1):
-            for d in (0, 1):
-                if (d, k, h) not in steps:
-                    continue
-                steps[d, k, h].wait_recv()
-                if k < 7 or (k == 7 and h == d):
-                    zsend(d, k + 1, h)
+            for part in (0, 1):
+                for d in (0, 1):
+                    if (d, k, h, part) not in steps:
+                        continue
+                    steps[d, k, h, part].wait_recv()
+                    slot = slot_r if d == 0 else slot_l
+                    if k == 8 or (k == 7 and h != d):
+                        continue
+                    if (slot(k + 1), h) not in PACKED:
+                        zsend(d, k + 1, h, part)
+                    elif part == len(blocks_of(slot(k), h)) - 1:
+                        zsend(d, k + 1, h, 0)
         if k == 1:
             for r in own_local:
                 r.wait()
@@ -299,23 +311,24 @@
     sends = []
     gots = {}
 
-    def zsend(d, k, h):
+    def zsend(d, k, h, part):
         slot = (slot_r if d == 0 else slot_l)(k)
-        rows = rows_of(slot, h)
-        r = remote(A.at[slot, h, rows], V.at[d, k - 1, h, rows], zs.at[d, k - 1, h], zr.at[d, k - 1, h], left if d == 0 else right)
+        rows = blocks_of(slot, h)[part]
+        at = (d, k - 1, h, part)
+        r = remote(A.at[slot, h, rows], V.at[d, k - 1, h, rows], zs.at[at], zr.at[at], left if d == 0 else right)
         r.start()
         sends.append(r)
-        gots[d, k - 1, h] = r
+        gots[d, k - 1, h, part] = r
 
     def msend(d, k):
         slot = (slot_r if d == 0 else slot_l)(k)
         r = remote(GA.at[slot], GV.at[d, k - 1], ms.at[d, k - 1], mr.at[d, k - 1], left if d == 0 else right)
         r.start()
         sends.append(r)
-        gots[d, k - 1, 2] = r
-
-    def add(slot, h, more, dst):
-        @pl.loop(0, TOK, step=32)
+        gots[d, k - 1, 2, 0] = r
+
+    def add(slot, h, part, more, dst):
+        @pl.loop(part * 64, part * 64 + 64, step=32)
         def _(at):
             rows = pl.ds(pl.multiple_of(at, 32), 32)
             total = A[slot, h, rows].astype(F32)
@@ -353,25 +366,28 @@
     unpack(0, True)
     for k in range(8, 0, -1):
         order = [(0, 1), (1, 0), (0, 0), (1, 1)] if k == 7 else [(0, 0), (1, 1)] if k == 8 else [(0, 0), (1, 0), (0, 1), (1, 1)]
-        for d, h in order:
+        for d, h, part in [(d, h, part) for h in (0, 1) for part in (0, 1) for d in (0, 1)] if k < 7 else [(d, h, 0) for d, h in order]:
             slot = (slot_r if d == 0 else slot_l)(k)
-            if (d, k, h) in gots:
-                gots[d, k, h].wait_recv()
-                came = PACKED.get(((slot_r if d == 0 else slot_l)(k + 1), h))
-                if came is None:
-                    add(slot, h, [(d, k)], A.at[slot, h])
-                elif came == 8:
+            far = ((slot_r if d == 0 else slot_l)(k + 1), h) if k < 8 else None
+            if part == len(blocks_of(slot, h)):
+                continue
+            if k < 7 and far not in PACKED:
+                gots[d, k, h, part].wait_recv()
+                add(slot, h, part, [(d, k)], A.at[slot, h])
+            elif part == 0 and (d, k, h, 0) in gots:
+                gots[d, k, h, 0].wait_recv()
+                if PACKED[far] == 8:
                     total = A[slot, h, 32:80].astype(F32) + V[d, k, h, 0:48].astype(F32)
                     A[slot, h, 32:80] = total.astype(BF)
                 else:
                     hot = ahead(M[slot], z, d)
                     total = lax.dot_general(hot, V[d, k, h, 0:80], (((0,), (0,)), ((), ())), preferred_element_type=F32)
                     A[slot, h] = (total + A[slot, h].astype(F32)).astype(BF)
-            zsend(d, k, h)
+            zsend(d, k, h, part)
         for d in (0, 1) if k < 8 else (0,):
             slot = (slot_r if d == 0 else slot_l)(k)
-            if (d, k, 2) in gots:
-                gots[d, k, 2].wait_recv()
+            if (d, k, 2, 0) in gots:
+                gots[d, k, 2, 0].wait_recv()
                 GA[slot] = add_gate(slot, [(d, k)])
             msend(d, k)
         if k > 1:
@@ -449,14 +465,15 @@
     for r in last:
         r.start()
     for h in (0, 1):
-        for d in (0, 1):
-            gots[d, 0, h].wait_recv()
-        add(0, h, [(0, 0), (1, 0)], FV.at[h])
+        for part in (0, 1):
+            for d in (0, 1):
+                gots[d, 0, h, part].wait_recv()
+            add(0, h, part, [(0, 0), (1, 0)], FV.at[h])
         r = pltpu.make_async_copy(FV.at[h], F.at[h], loc.at[13 + h])
         r.start()
         last.append(r)
     for d in (0, 1):
-        gots[d, 0, 2].wait_recv()
+        gots[d, 0, 2, 0].wait_recv()
     GF[...] = add_gate(0, [(0, 0), (1, 0)])
     r = pltpu.make_async_copy(GF, GO, loc.at[15])
     r.start()
@@ -491,7 +508,7 @@
         in_specs=[ANY, ANY, VM, VM, ANY, ANY],
         out_specs=[ANY] * 4,
         scratch_shapes=[vm((NZ, 2, TOK, D), BF), vm((NZ, 16, TOK), BF), vm((8, 2, 3, NY, 16, D), BF), vm((4, 80, D), BF)]
-        + [dma((2, 8, 2))] * 2 + [dma((2, 8))] * 2 + [dma((8,))] * 3 + [dma((14,))] * 2 + [dma((5,))],
+        + [dma((2, 8, 2, 2))] * 2 + [dma((2, 8))] * 2 + [dma((8,))] * 3 + [dma((14,))] * 2 + [dma((5,))],
         compiler_params=pltpu.CompilerParams(collective_id=1, has_side_effects=True, vmem_limit_bytes=60 << 20),
     )(tokens, out_grad, expert_ids.T, gates.T, w_up, w_down)
 
@@ -514,7 +531,7 @@
             vm((NZ, 16, TOK), BF), vm((2, 8, 16, TOK), BF), vm((2, TOK, D), BF), vm((16, TOK), BF),
             vm((3, D, FF), BF), vm((D, FF), BF), vm((3, 256, FF), BF), vm((256, FF), BF), vm((128, FF), BF),
             vm((3, NY, FF, 256), BF), vm((NY, FF, 256), BF), vm((NY, FF, 256), BF), vm((3, FF, 256), BF), vm((FF, 256), BF), vm((FF, 128), BF),
-        ] + [dma((2, 8, 2))] * 2 + [dma((2, 8))] * 2 + [dma((8,))] * 2 + [dma((14,))] * 2 + [dma((16,)), dma((NY, 3))],
+        ] + [dma((2, 8, 2, 2))] * 2 + [dma((2, 8))] * 2 + [dma((8,))] * 2 + [dma((14,))] * 2 + [dma((16,)), dma((NY, 3))],
         compiler_params=pltpu.CompilerParams(collective_id=2, has_side_effects=True, vmem_limit_bytes=60 << 20),
     )(X, M, WU, WD)
 

time: 192 us -> 193 us (level)
  no operation moved by 1% of the time
where the time goes in v6:
time: 193 us
  Pallas kernels  192 us (99%)
    pallas_call x1, Pallas kernels, shards(): pl.pallas_call(ag_kernel, name='gather', out_shape=(sd((3, NY, 256, D), B...  97.1 us
    pallas_call x1, Pallas kernels, shards(): pl.pallas_call(rs_kernel, name='scatter', out_shape=(sd((2, TOK, D), BF),...  92.6 us

profile of v6, /device:TPU:1, one launch (start us, length us, event | category | flops | bytes accessed | tf_op | source)
XLA Modules:
  0.0 192.7 jit_solution(11132889836257746534)
XLA Ops:
  0.6 97.1 %gather.1 = (bf16[3,4,256,1024]{3,2,1,0:T(8,128)(2,1)}, bf16[16,16,128]{2,1,0:T(8,128)(2,1)}, bf16[4,1024,512]{2,1,0:T(8,128)(2,1)}, bf16[4,512,1024]{2,1,0:T(8,128)(2,1)}) custom-call(bf16[128,1024]{1,0:T(8,128)(2,1)} %tok.1, bf16[128,1024]{1,0:T(8,128)(2,1)} %cot.1, s32[4,128]{1,0:T(4,128)} %bitcast.3, bf16[4,128]{1,0:T(4,128)(2,1)} %bitcast.4, ...), custom_call_target="tpu_custom_call" | custom-call | tf_op jit(solution)/shard_map/gather/pallas_call | solution.py:499
  97.8 92.6 %scatter.1 = (bf16[2,128,1024]{2,1,0:T(8,128)(2,1)}, bf16[16,128]{1,0:T(8,128)(2,1)}, bf16[2,128,512]{2,1,0:T(8,128)(2,1)}, bf16[2,512,128]{2,1,0:T(8,128)(2,1)}) custom-call(bf16[3,4,256,1024]{3,2,1,0:T(8,128)(2,1)} %get-tuple-element.18.X, bf16[16,16,128]{2,1,0:T(8,128)(2,1)} %get-tuple-element.19.MI, bf16[4,1024,512]{2,1,0:T(8,128)(2,1)} %get-tuple-element.20.WU, ...), custom_call_target="tpu_custom_call" | custom-call | tf_op jit(solution)/shard_map/scatter/pallas_call | solution.py:515
  190.4 2.4 %outputs.1 = (bf16[128,1024]{1,0:T(8,128)(2,1)}, bf16[128,1024]{1,0:T(8,128)(2,1)}, bf16[4,128]{1,0:T(4,128)(2,1)}, f32[2,128,512]{2,1,0:T(8,128)}, f32[2,512,128]{2,1,0:T(8,128)}) custom-call(bf16[2,128,1024]{2,1,0:T(8,128)(2,1)} %get-tuple-element.22.F, bf16[16,128]{1,0:T(8,128)(2,1)} %get-tuple-element.23.G, bf16[2,128,512]{2,1,0:T(8,128)(2,1)} %get-tuple-element.24.UG, ...), custom_call_target="tpu_custom_call" | custom-call | tf_op jit(solution)/shard_map/outputs/pallas_call | solution.py:538

commit v7 on v5

--- a/solution.py
+++ b/solution.py
@@ -113,12 +113,12 @@
     own = (tok, cot)
     steps = {}
 
-    def zsend(d, k, h):
+    def zsend(d, k, h, hot=None):
         slot = slot_r if d == 0 else slot_l
         kind, rows = PACKED.get((slot(k), h)), rows_of(slot(k), h)
         if kind == 0:
             past, n = slot(k - 1), 2 * d + k - 6
-            Q[n] = jnp.dot(ahead(M[past], z, d), T[past, h], preferred_element_type=F32).astype(BF)
+            Q[n] = jnp.dot(hot, T[past, h], preferred_element_type=F32).astype(BF)
             src = Q.at[n]
         elif kind == 8:
             src = T.at[slot(k - 1), h, pl.ds(32, 48)]
@@ -207,13 +207,14 @@
             if k < 7 or (k == 7 and d == 0):
                 msend(d, k + 1)
         chosen = choose(0) if k == 8 else None
+        hots = [ahead(M[2 * k - 1 + d], z, d) if k in (5, 6) else None for d in (0, 1)]
         for h in (0, 1):
             for d in (0, 1):
                 if (d, k, h) not in steps:
                     continue
                 steps[d, k, h].wait_recv()
                 if k < 7 or (k == 7 and h == d):
-                    zsend(d, k + 1, h)
+                    zsend(d, k + 1, h, hots[d])
         if k == 1:
             for r in own_local:
                 r.wait()
@@ -329,16 +330,17 @@
             total += GV[d, k].astype(F32)
         return total.astype(BF)
 
-    def unpack(p, first=False):
+    def choose(p):
         slots = pair_slots(p)
         hot, weight, eqs = selection(M[slots[0]], M[slots[1]], z * 8, c)
+        gate = jnp.sum(weight, axis=1, keepdims=True)
+        return (routes(slots, 0, weight, c, gate), routes(slots, 1, hot, c)), eqs
+
+    def unpack(p, chosen):
+        slots = pair_slots(p)
+        ways, eqs = chosen
         rows = pl.ds(p * 16, 16)
         over = (((0,), (0,)), ((), ()))
-        gate = jnp.sum(weight, axis=1, keepdims=True)
-        ways = (routes(slots, 0, weight, c, gate), routes(slots, 1, hot, c))
-        if first:
-            for r in core:
-                r.wait_recv()
         for n, w in enumerate(ways):
             v = jnp.concatenate([b[n, q, rows] for b in (OB, OR) for q in range(NY)], axis=0)
             u = lax.dot_general(w, v, over, preferred_element_type=F32).astype(BF)
@@ -350,7 +352,10 @@
             GA[slot] = jnp.concatenate(gp + [jnp.zeros((12, TOK), F32)], axis=0).astype(BF)
 
     near.wait()
-    unpack(0, True)
+    chosen, second = choose(0), choose(7)
+    for r in core:
+        r.wait_recv()
+    unpack(0, chosen)
     for k in range(8, 0, -1):
         order = [(0, 1), (1, 0), (0, 0), (1, 1)] if k == 7 else [(0, 0), (1, 1)] if k == 8 else [(0, 0), (1, 0), (0, 1), (1, 1)]
         for d, h in order:
@@ -364,8 +369,7 @@
                     total = A[slot, h, 32:80].astype(F32) + V[d, k, h, 0:48].astype(F32)
                     A[slot, h, 32:80] = total.astype(BF)
                 else:
-                    hot = ahead(M[slot], z, d)
-                    total = lax.dot_general(hot, V[d, k, h, 0:80], (((0,), (0,)), ((), ())), preferred_element_type=F32)
+                    total = lax.dot_general(hots[d], V[d, k, h, 0:80], (((0,), (0,)), ((), ())), preferred_element_type=F32)
                     A[slot, h] = (total + A[slot, h].astype(F32)).astype(BF)
             zsend(d, k, h)
         for d in (0, 1) if k < 8 else (0,):
@@ -375,7 +379,8 @@
                 GA[slot] = add_gate(slot, [(d, k)])
             msend(d, k)
         if k > 1:
-            unpack(k - 1)
+            unpack(k - 1, second if k == 8 else choose(k - 1))
+        hots = [ahead(M[2 * k - 3 + d], z, d) if k in (7, 6) else None for d in (0, 1)]
         if k in (7, 6):
             weigh(2 * (7 - k))
             weigh(2 * (7 - k) + 1)

time: 192 us -> 192 us (level)
  no operation moved by 1% of the time
where the time goes in v7:
time: 192 us
  Pallas kernels  191 us (99%)
    pallas_call x1, Pallas kernels, shards(): pl.pallas_call(ag_kernel, name='gather', out_shape=(sd((3, NY, 256, D), B...  96.5 us
    pallas_call x1, Pallas kernels, shards(): pl.pallas_call(rs_kernel, name='scatter', out_shape=(sd((2, TOK, D), BF),...  92.2 us

profile of v7, /device:TPU:1, one launch (start us, length us, event | category | flops | bytes accessed | tf_op | source)
XLA Modules:
  0.0 191.7 jit_solution(6874542981984240265)
XLA Ops:
  0.6 96.5 %gather.1 = (bf16[3,4,256,1024]{3,2,1,0:T(8,128)(2,1)}, bf16[16,16,128]{2,1,0:T(8,128)(2,1)}, bf16[4,1024,512]{2,1,0:T(8,128)(2,1)}, bf16[4,512,1024]{2,1,0:T(8,128)(2,1)}) custom-call(bf16[128,1024]{1,0:T(8,128)(2,1)} %tok.1, bf16[128,1024]{1,0:T(8,128)(2,1)} %cot.1, s32[4,128]{1,0:T(4,128)} %bitcast.3, bf16[4,128]{1,0:T(4,128)(2,1)} %bitcast.4, ...), custom_call_target="tpu_custom_call" | custom-call | tf_op jit(solution)/shard_map/gather/pallas_call | solution.py:487
  97.2 92.2 %scatter.1 = (bf16[2,128,1024]{2,1,0:T(8,128)(2,1)}, bf16[16,128]{1,0:T(8,128)(2,1)}, bf16[2,128,512]{2,1,0:T(8,128)(2,1)}, bf16[2,512,128]{2,1,0:T(8,128)(2,1)}) custom-call(bf16[3,4,256,1024]{3,2,1,0:T(8,128)(2,1)} %get-tuple-element.18.X, bf16[16,16,128]{2,1,0:T(8,128)(2,1)} %get-tuple-element.19.MI, bf16[4,1024,512]{2,1,0:T(8,128)(2,1)} %get-tuple-element.20.WU, ...), custom_call_target="tpu_custom_call" | custom-call | tf_op jit(solution)/shard_map/scatter/pallas_call | solution.py:503
  189.4 2.4 %outputs.1 = (bf16[128,1024]{1,0:T(8,128)(2,1)}, bf16[128,1024]{1,0:T(8,128)(2,1)}, bf16[4,128]{1,0:T(4,128)(2,1)}, f32[2,128,512]{2,1,0:T(8,128)}, f32[2,512,128]{2,1,0:T(8,128)}) custom-call(bf16[2,128,1024]{2,1,0:T(8,128)(2,1)} %get-tuple-element.22.F, bf16[16,128]{1,0:T(8,128)(2,1)} %get-tuple-element.23.G, bf16[2,128,512]{2,1,0:T(8,128)(2,1)} %get-tuple-element.24.UG, ...), custom_call_target="tpu_custom_call" | custom-call | tf_op jit(solution)/shard_map/outputs/pallas_call | solution.py:526
